TPU v7x, 32 devices: a whole 2x2x4 slice. The times are simulated.
32 devices in a mesh: seq: 8 (over z, core), head: 4 (over y, x).
Axes of the slice: x: 2, y: 2, z: 4, core: 2. Of those that a mesh axis runs over, the one named last changes fastest.
Arguments:
- queries: bfloat16 [2048, 16, 128], P(('seq', 'head')), may hold values from -6 to 6
- keys: bfloat16 [2048, 16, 128], P(('seq', 'head')), may hold values from -6 to 6
- values: bfloat16 [2048, 16, 128], P(('seq', 'head')), may hold values from -6 to 6
- log_decay: bfloat16 [2048, 16], P(('seq', 'head')), may hold values from -1 to 0
- beta: bfloat16 [2048, 16], P(('seq', 'head')), may hold values from 0.0099 to 0.6
- norm_gain: float32 [128], replicated, may hold values from 0.25 to 1.75
Outputs:
- normed_core: bfloat16 [2048, 16, 128], P(('seq', 'head'))
All inputs are finite; a program needn't handle non-finite values.
Results may differ from a plain program's by a relative error of at most 0.013.
Values may be sent and summed in bfloat16 or wider, within the bound.
A program may use at most 64 MiB of HBM per device.

v0:
```python
import jax
import jax.numpy as jnp
from jax import lax
from jax.sharding import PartitionSpec as P

GROUP = 64


HIGH = lax.Precision.HIGHEST


def from_behind(value, axis, steps):
    count = lax.axis_size(axis)
    initial, last = (max(0, -steps), min(count, count - steps))
    return lax.ppermute(value, axis, [(source, source + steps) for source in range(initial, last)])


def unit_rows(tensor):
    tensor = tensor.astype(jnp.float32)
    return tensor * lax.rsqrt(jnp.sum(tensor * tensor, axis=-1, keepdims=True) + 1e-06)


def multiply(left, right):
    return jnp.einsum("...ij,...jk->...ik", left, right, precision=HIGH)


def compose(earlier, later):
    return (multiply(later[0], earlier[0]), multiply(later[0], earlier[1]) + later[1])


def grouped(tensor):
    token_count, head_count, head_width = tensor.shape
    return tensor.reshape(token_count // GROUP, GROUP, head_count, head_width).transpose(2, 0, 1, 3)


def grouped_gate(tensor):
    token_count, head_count = tensor.shape
    return (
        tensor.astype(jnp.float32)
        .reshape(token_count // GROUP, GROUP, head_count)
        .transpose(2, 0, 1)
    )


def key_terms(group_keys, group_values, group_gates, group_betas):
    cumulative = jnp.cumsum(group_gates, axis=-1)
    row_ids = lax.broadcasted_iota(jnp.int32, (GROUP, GROUP), 0)
    col_ids = lax.broadcasted_iota(jnp.int32, (GROUP, GROUP), 1)
    within = row_ids >= col_ids
    spread = jnp.where(
        within,
        jnp.exp(jnp.where(within, cumulative[..., :, None] - cumulative[..., None, :], 0.0)),
        0.0,
    )
    intersection = jnp.einsum(
        "...id,...jd->...ij", group_keys, group_keys, preferred_element_type=jnp.float32
    )
    keys_wide = group_keys.astype(jnp.float32)
    lower_part = (
        jnp.where(row_ids > col_ids, intersection * spread, 0.0) * group_betas[..., :, None]
    )
    system = lower_part + jnp.eye(GROUP, dtype=jnp.float32)
    scaled = (
        jnp.concatenate([group_values, keys_wide * jnp.exp(cumulative)[..., None]], axis=-1)
        * group_betas[..., None]
    )
    solved = jax.scipy.linalg.solve_triangular(system, scaled, lower=True, unit_diagonal=True)
    head_width = group_keys.shape[-1]
    pseudo = solved[..., :head_width]
    erasers = solved[..., head_width:]
    final_log = cumulative[..., -1:]
    carried = keys_wide * jnp.exp(final_log - cumulative)[..., None]
    return (cumulative, spread, pseudo, erasers, carried, jnp.exp(final_log[..., 0]))


def local(queries, keys, values, log_decay, beta, norm_gain):
    head_queries, head_keys, head_values, head_gates, head_betas = (
        lax.all_to_all(queries, "head", split_axis=1, concat_axis=0, tiled=True),
        lax.all_to_all(keys, "head", split_axis=1, concat_axis=0, tiled=True),
        lax.all_to_all(values, "head", split_axis=1, concat_axis=0, tiled=True),
        lax.all_to_all(log_decay, "head", split_axis=1, concat_axis=0, tiled=True),
        lax.all_to_all(beta, "head", split_axis=1, concat_axis=0, tiled=True),
    )
    token_count, head_count, head_width = head_keys.shape
    group_keys = grouped(unit_rows(head_keys).astype(jnp.bfloat16))
    group_values = grouped(head_values.astype(jnp.float32))
    cumulative, spread, pseudo, erasers, carried, decays = key_terms(
        group_keys, group_values, grouped_gate(head_gates), grouped_gate(head_betas)
    )
    identity = jnp.eye(head_width, dtype=jnp.float32)
    linear_maps = decays[..., None, None] * identity - jnp.einsum(
        "...cd,...ce->...de", carried, erasers, precision=HIGH
    )
    offset_maps = jnp.einsum("...cd,...ce->...de", carried, pseudo, precision=HIGH)
    sections = []
    while linear_maps.shape[1] > 1:
        sections.append((linear_maps, offset_maps))
        linear_maps, offset_maps = compose(
            (linear_maps[:, 0::2], offset_maps[:, 0::2]),
            (linear_maps[:, 1::2], offset_maps[:, 1::2]),
        )
    slab_linear = linear_maps[:, 0]
    slab_offset = offset_maps[:, 0]
    group_queries = grouped((unit_rows(head_queries) * head_width ** (-0.5)).astype(jnp.bfloat16))
    scores = (
        jnp.einsum(
            "...id,...jd->...ij", group_queries, group_keys, preferred_element_type=jnp.float32
        )
        * spread
    )
    gated_queries = group_queries.astype(jnp.float32) * jnp.exp(cumulative)[..., None]
    zero_state = jnp.zeros((head_count, head_width, head_width), jnp.float32)

    def relay(counter, incoming):
        outgoing = multiply(slab_linear, incoming) + slab_offset
        return from_behind(outgoing, "seq", 1)

    entry = lax.fori_loop(0, lax.axis_size("seq") - 1, relay, zero_state)
    states = entry[:, None]
    for section_linear, section_offset in reversed(sections):
        odd_states = multiply(section_linear[:, 0::2], states) + section_offset[:, 0::2]
        states = jnp.stack([states, odd_states], axis=2).reshape(section_linear.shape)
    residue = pseudo - multiply(erasers, states)
    core = multiply(gated_queries, states) + jnp.einsum(
        "...ij,...je->...ie", scores, residue, precision=HIGH
    )
    scale_rows = lax.rsqrt(jnp.mean(core * core, axis=-1, keepdims=True) + 1e-06)
    normed = (core * scale_rows * norm_gain).astype(jnp.bfloat16)
    normed = normed.transpose(1, 2, 0, 3).reshape(token_count, head_count, head_width)
    return lax.all_to_all(normed, "head", split_axis=0, concat_axis=1, tiled=True)


def solution(mesh):
    placed = (
        P(("seq", "head"), None, None),
        P(("seq", "head"), None, None),
        P(("seq", "head"), None, None),
        P(("seq", "head"), None),
        P(("seq", "head"), None),
        P(),
    )
    return jax.shard_map(
        local, mesh=mesh, in_specs=placed, out_specs=P(("seq", "head"), None, None), check_vma=False
    )
```

profile of v0, /device:TPU:24, one launch (start us, length us, event | category | flops | bytes accessed | tf_op | source)
XLA Modules:
  0.0 196.7 jit_solution(15544907358524818347)
XLA Ops:
  0.0 1.4 reshape.133
  1.4 3.7 %all-to-all-start.1 = ((bf16[4,2,128]{2,1,0:T(2,128)(2,1)}), bf16[4,2,128]{2,1,0:T(2,128)(2,1)S(1)}, u32[]{:S(2)}, u32[]{:S(2)}) async-start(bf16[4,2,128]{2,1,0:T(2,128)(2,1)} %reshape.133), calls=%async_computation.1 | async-start | bytes 4096 | tf_op jit(solution)/shard_map/all_to_all | solution.py:81
  5.2 1.8 copy.61
  9.6 4.0 %all-to-all-start.3 = ((bf16[4,2,128]{2,1,0:T(2,128)(2,1)}), bf16[4,2,128]{2,1,0:T(2,128)(2,1)S(1)}, u32[]{:S(2)}, u32[]{:S(2)}) async-start(bf16[4,2,128]{2,1,0:T(2,128)(2,1)} %reshape.135), calls=%async_computation.3 | async-start | bytes 4096 | tf_op jit(solution)/shard_map/all_to_all | solution.py:82
  14.8 3.4 %all-to-all-done.3 = bf16[4,2,128]{2,1,0:T(2,128)(2,1)S(1)} async-done(((bf16[4,2,128]{2,1,0:T(2,128)(2,1)}), bf16[4,2,128]{2,1,0:T(2,128)(2,1)S(1)}, u32[]{:S(2)}, u32[]{:S(2)}) %all-to-all-start.3) | async-done | bytes 2080 | tf_op jit(solution)/shard_map/all_to_all | solution.py:82
  18.2 3.4 %all-to-all-start.2 = ((bf16[64,16,128]{2,0,1:T(8,128)(2,1)}), bf16[64,16,128]{2,0,1:T(8,128)(2,1)S(1)}, u32[]{:S(2)}, u32[]{:S(2)}) async-start(bf16[64,16,128]{2,0,1:T(8,128)(2,1)} %copy.61), calls=%async_computation.2 | async-start | bytes 524288 | tf_op jit(solution)/shard_map/all_to_all | solution.py:79
  21.8 5.2 %all-to-all-done.2 = bf16[64,16,128]{2,0,1:T(8,128)(2,1)S(1)} async-done(((bf16[64,16,128]{2,0,1:T(8,128)(2,1)}), bf16[64,16,128]{2,0,1:T(8,128)(2,1)S(1)}, u32[]{:S(2)}, u32[]{:S(2)}) %all-to-all-start.2) | async-done | bytes 262176 | tf_op jit(solution)/shard_map/all_to_all | solution.py:79
  27.0 3.4 %all-to-all-start.4 = ((bf16[64,16,128]{2,0,1:T(8,128)(2,1)}), bf16[64,16,128]{2,0,1:T(8,128)(2,1)S(1)}, u32[]{:S(2)}, u32[]{:S(2)}) async-start(bf16[64,16,128]{2,0,1:T(8,128)(2,1)} %copy.67), calls=%async_computation.4 | async-start | bytes 524288 | tf_op jit(solution)/shard_map/all_to_all | solution.py:80
  31.3 78.6 %custom-call.4 = f32[4,4,1,64,64]{3,4,2,1,0:T(8,128)S(1)} custom-call(f32[4,4,1,64,64]{4,3,2,1,0:T(8,128)S(1)} %fusion.6), custom_call_target="InvertDiagBlocksLowerTriangular" | custom-call | tf_op jit(solution)/shard_map/jit(_solve_triangular)/vmap(vmap())/triangular_solve | solution.py:67
  110.0 4.2 %all-to-all-start = ((bf16[64,16,128]{2,0,1:T(8,128)(2,1)}), bf16[64,16,128]{2,0,1:T(8,128)(2,1)S(1)}, u32[]{:S(2)}, u32[]{:S(2)}) async-start(bf16[64,16,128]{2,0,1:T(8,128)(2,1)} %copy.55), calls=%async_computation | async-start | bytes 524288 | tf_op jit(solution)/shard_map/all_to_all | solution.py:78
  114.2 1.2 fusion.11
  115.5 2.0 %fusion.14 = f32[4,4,128,128]{3,2,1,0:T(8,128)S(1)} fusion(bf16[4,4,64,128]{3,2,1,0:T(8,128)(2,1)S(1)} %get-tuple-element.37, f32[4,4,64,256]{3,2,1,0:T(8,128)S(1)} %fusion.11, f32[4,4,64]{2,1,0:T(4,128)S(1)} %get-tuple-element.38), kind=kOutput, calls=%fused_computation.28 | convolution fusion | flops 201588736 | bytes 1843200 | tf_op jit(solution)/shard_map/...cd,...ce->...de/dot_general | solution.py:94
  117.5 2.0 %convolution_subtract_fusion = f32[4,4,128,128]{3,2,1,0:T(8,128)S(1)} fusion(bf16[4,4,64,128]{3,2,1,0:T(8,128)(2,1)S(1)} %get-tuple-element.37, f32[128,128]{1,0:T(8,128)S(1)} %fusion.39, f32[4,4]{1,0:T(4,128)S(1)} %exp.26, f32[4,4,64,256]{3,2,1,0:T(8,128)S(1)} %fusion.11, f32[4,4,64]{2,1,0:T(4,128)S(1)} %get-tuple-element.38), kind=kOutput, calls=%fused_computation.1 | convolution fusion | flops 202113024 | bytes 1910784 | tf_op jit(solution)/shard_map/...cd,...ce->...de/dot_general | solution.py:91
  121.7 56.7 %while.10 = (s32[]{:T(128)}, f32[4,128,128]{2,1,0:T(8,128)S(1)}, f32[4,128,128]{2,1,0:T(8,128)S(1)}, f32[4,128,128]{2,1,0:T(8,128)S(1)}, s32[]{:T(128)}) while((s32[]{:T(128)}, f32[4,128,128]{2,1,0:T(8,128)S(1)}, f32[4,128,128]{2,1,0:T(8,128)S(1)}, f32[4,128,128]{2,1,0:T(8,128)S(1)}, s32[]{:T(128)}) %tuple.23), condition=%wide.region_4.5_spmd, body=%wide.region_3.4_spmd.sunk | while | flops 100728832 | bytes 2097253 | solution.py:118
  122.1 1.9 collective-permute-start
  124.1 5.8 %collective-permute-done = f32[4,128,128]{2,1,0:T(8,128)S(1)} collective-permute-done((f32[4,128,128]{2,1,0:T(8,128)S(1)}, f32[4,128,128]{2,1,0:T(8,128)S(1)}, u32[]{:S(2)}, u32[]{:S(2)}) %collective-permute-start) | collective-permute-done | bytes 262176 | tf_op jit(solution)/shard_map/while/body/eval_jaxpr/ppermute | solution.py:15
  130.2 1.9 collective-permute-start
  132.2 5.8 %collective-permute-done = f32[4,128,128]{2,1,0:T(8,128)S(1)} collective-permute-done((f32[4,128,128]{2,1,0:T(8,128)S(1)}, f32[4,128,128]{2,1,0:T(8,128)S(1)}, u32[]{:S(2)}, u32[]{:S(2)}) %collective-permute-start) | collective-permute-done | bytes 262176 | tf_op jit(solution)/shard_map/while/body/eval_jaxpr/ppermute | solution.py:15
  138.3 1.9 collective-permute-start
  140.2 5.8 %collective-permute-done = f32[4,128,128]{2,1,0:T(8,128)S(1)} collective-permute-done((f32[4,128,128]{2,1,0:T(8,128)S(1)}, f32[4,128,128]{2,1,0:T(8,128)S(1)}, u32[]{:S(2)}, u32[]{:S(2)}) %collective-permute-start) | collective-permute-done | bytes 262176 | tf_op jit(solution)/shard_map/while/body/eval_jaxpr/ppermute | solution.py:15
  146.4 1.9 collective-permute-start
  148.3 5.8 %collective-permute-done = f32[4,128,128]{2,1,0:T(8,128)S(1)} collective-permute-done((f32[4,128,128]{2,1,0:T(8,128)S(1)}, f32[4,128,128]{2,1,0:T(8,128)S(1)}, u32[]{:S(2)}, u32[]{:S(2)}) %collective-permute-start) | collective-permute-done | bytes 262176 | tf_op jit(solution)/shard_map/while/body/eval_jaxpr/ppermute | solution.py:15
  154.5 1.9 collective-permute-start
  156.4 5.8 %collective-permute-done = f32[4,128,128]{2,1,0:T(8,128)S(1)} collective-permute-done((f32[4,128,128]{2,1,0:T(8,128)S(1)}, f32[4,128,128]{2,1,0:T(8,128)S(1)}, u32[]{:S(2)}, u32[]{:S(2)}) %collective-permute-start) | collective-permute-done | bytes 262176 | tf_op jit(solution)/shard_map/while/body/eval_jaxpr/ppermute | solution.py:15
  162.6 1.9 collective-permute-start
  164.5 5.8 %collective-permute-done = f32[4,128,128]{2,1,0:T(8,128)S(1)} collective-permute-done((f32[4,128,128]{2,1,0:T(8,128)S(1)}, f32[4,128,128]{2,1,0:T(8,128)S(1)}, u32[]{:S(2)}, u32[]{:S(2)}) %collective-permute-start) | collective-permute-done | bytes 262176 | tf_op jit(solution)/shard_map/while/body/eval_jaxpr/ppermute | solution.py:15
  170.7 1.9 collective-permute-start
  172.6 5.8 %collective-permute-done = f32[4,128,128]{2,1,0:T(8,128)S(1)} collective-permute-done((f32[4,128,128]{2,1,0:T(8,128)S(1)}, f32[4,128,128]{2,1,0:T(8,128)S(1)}, u32[]{:S(2)}, u32[]{:S(2)}) %collective-permute-start) | collective-permute-done | bytes 262176 | tf_op jit(solution)/shard_map/while/body/eval_jaxpr/ppermute | solution.py:15
  178.4 1.5 fusion.10
  180.8 1.1 convolution_subtract_fusion.1
  183.8 1.3 multiply_reduce_fusion
  186.2 9.7 %all_to_all.71 = bf16[256,4,128]{2,1,0:T(4,128)(2,1)S(1)} all-to-all(bf16[256,4,128]{2,1,0:T(4,128)(2,1)S(1)} %copy.76), channel_id=1, replica_groups=mesh['seq'=8,'head'=4] {'head'}, dimensions={0} | all-to-all | bytes 524288 | tf_op jit(solution)/shard_map/all_to_all | solution.py:130
  (72 shorter events, 14.5 us)
Async XLA Ops:
  1.4 8.2 %all-to-all-start.1 = ((bf16[4,2,128]{2,1,0:T(2,128)(2,1)}), bf16[4,2,128]{2,1,0:T(2,128)(2,1)S(1)}, u32[]{:S(2)}, u32[]{:S(2)}) async-start(bf16[4,2,128]{2,1,0:T(2,128)(2,1)} %reshape.133), calls=%async_computation.1 | async-start | bytes 4096 | tf_op jit(solution)/shard_map/all_to_all | solution.py:81
  5.2 1.8 copy-start.8
  5.2 2.4 %copy-start.6 = (bf16[64,16,128]{2,1,0:T(8,128)(2,1)S(1)}, bf16[64,16,128]{2,1,0:T(8,128)(2,1)}, u32[]{:S(2)}) copy-start(bf16[64,16,128]{2,1,0:T(8,128)(2,1)} %param.10) | copy-start | bytes 786436
  7.7 1.0 copy-start.7
  9.6 8.6 %all-to-all-start.3 = ((bf16[4,2,128]{2,1,0:T(2,128)(2,1)}), bf16[4,2,128]{2,1,0:T(2,128)(2,1)S(1)}, u32[]{:S(2)}, u32[]{:S(2)}) async-start(bf16[4,2,128]{2,1,0:T(2,128)(2,1)} %reshape.135), calls=%async_computation.3 | async-start | bytes 4096 | tf_op jit(solution)/shard_map/all_to_all | solution.py:82
  18.2 8.8 %all-to-all-start.2 = ((bf16[64,16,128]{2,0,1:T(8,128)(2,1)}), bf16[64,16,128]{2,0,1:T(8,128)(2,1)S(1)}, u32[]{:S(2)}, u32[]{:S(2)}) async-start(bf16[64,16,128]{2,0,1:T(8,128)(2,1)} %copy.61), calls=%async_computation.2 | async-start | bytes 524288 | tf_op jit(solution)/shard_map/all_to_all | solution.py:79
  27.0 83.0 %all-to-all-start.4 = ((bf16[64,16,128]{2,0,1:T(8,128)(2,1)}), bf16[64,16,128]{2,0,1:T(8,128)(2,1)S(1)}, u32[]{:S(2)}, u32[]{:S(2)}) async-start(bf16[64,16,128]{2,0,1:T(8,128)(2,1)} %copy.67), calls=%async_computation.4 | async-start | bytes 524288 | tf_op jit(solution)/shard_map/all_to_all | solution.py:80
  31.0 86.5 %copy-start.3 = (bf16[4,4,64,128]{3,2,1,0:T(8,128)(2,1)}, bf16[4,4,64,128]{3,2,1,0:T(8,128)(2,1)S(1)}, u32[]{:S(2)}) copy-start(bf16[4,4,64,128]{3,2,1,0:T(8,128)(2,1)S(1)} %get-tuple-element.37) | copy-start | bytes 786436
  110.0 71.8 %all-to-all-start = ((bf16[64,16,128]{2,0,1:T(8,128)(2,1)}), bf16[64,16,128]{2,0,1:T(8,128)(2,1)S(1)}, u32[]{:S(2)}, u32[]{:S(2)}) async-start(bf16[64,16,128]{2,0,1:T(8,128)(2,1)} %copy.55), calls=%async_computation | async-start | bytes 524288 | tf_op jit(solution)/shard_map/all_to_all | solution.py:78
  117.5 2.7 %copy-start.1 = (f32[4,4,128,128]{3,2,1,0:T(8,128)}, f32[4,4,128,128]{3,2,1,0:T(8,128)S(1)}, u32[]{:S(2)}) copy-start(f32[4,4,128,128]{3,2,1,0:T(8,128)S(1)} %fusion.14) | copy-start | bytes 3145732
  120.2 1.1 copy-start
  120.9 0.8 copy-start.5
  122.1 7.7 %collective-permute-start = (f32[4,128,128]{2,1,0:T(8,128)S(1)}, f32[4,128,128]{2,1,0:T(8,128)S(1)}, u32[]{:S(2)}, u32[]{:S(2)}) collective-permute-start(f32[4,128,128]{2,1,0:T(8,128)S(1)} %convolution_add_fusion.5), channel_id=1, source_target_pairs={{0,4},{4,8},{8,12},{12,16},{16,20},{20,24},{24,28},{1,5},{5,9},{9,... | collective-permute-start | bytes 786440 | tf_op jit(solution)/shard_map/while/body/eval_jaxpr/ppermute | solution.py:15
  130.2 7.7 %collective-permute-start = (f32[4,128,128]{2,1,0:T(8,128)S(1)}, f32[4,128,128]{2,1,0:T(8,128)S(1)}, u32[]{:S(2)}, u32[]{:S(2)}) collective-permute-start(f32[4,128,128]{2,1,0:T(8,128)S(1)} %convolution_add_fusion.5), channel_id=1, source_target_pairs={{0,4},{4,8},{8,12},{12,16},{16,20},{20,24},{24,28},{1,5},{5,9},{9,... | collective-permute-start | bytes 786440 | tf_op jit(solution)/shard_map/while/body/eval_jaxpr/ppermute | solution.py:15
  138.3 7.7 %collective-permute-start = (f32[4,128,128]{2,1,0:T(8,128)S(1)}, f32[4,128,128]{2,1,0:T(8,128)S(1)}, u32[]{:S(2)}, u32[]{:S(2)}) collective-permute-start(f32[4,128,128]{2,1,0:T(8,128)S(1)} %convolution_add_fusion.5), channel_id=1, source_target_pairs={{0,4},{4,8},{8,12},{12,16},{16,20},{20,24},{24,28},{1,5},{5,9},{9,... | collective-permute-start | bytes 786440 | tf_op jit(solution)/shard_map/while/body/eval_jaxpr/ppermute | solution.py:15
  146.4 7.7 %collective-permute-start = (f32[4,128,128]{2,1,0:T(8,128)S(1)}, f32[4,128,128]{2,1,0:T(8,128)S(1)}, u32[]{:S(2)}, u32[]{:S(2)}) collective-permute-start(f32[4,128,128]{2,1,0:T(8,128)S(1)} %convolution_add_fusion.5), channel_id=1, source_target_pairs={{0,4},{4,8},{8,12},{12,16},{16,20},{20,24},{24,28},{1,5},{5,9},{9,... | collective-permute-start | bytes 786440 | tf_op jit(solution)/shard_map/while/body/eval_jaxpr/ppermute | solution.py:15
  154.5 7.7 %collective-permute-start = (f32[4,128,128]{2,1,0:T(8,128)S(1)}, f32[4,128,128]{2,1,0:T(8,128)S(1)}, u32[]{:S(2)}, u32[]{:S(2)}) collective-permute-start(f32[4,128,128]{2,1,0:T(8,128)S(1)} %convolution_add_fusion.5), channel_id=1, source_target_pairs={{0,4},{4,8},{8,12},{12,16},{16,20},{20,24},{24,28},{1,5},{5,9},{9,... | collective-permute-start | bytes 786440 | tf_op jit(solution)/shard_map/while/body/eval_jaxpr/ppermute | solution.py:15
  162.6 7.7 %collective-permute-start = (f32[4,128,128]{2,1,0:T(8,128)S(1)}, f32[4,128,128]{2,1,0:T(8,128)S(1)}, u32[]{:S(2)}, u32[]{:S(2)}) collective-permute-start(f32[4,128,128]{2,1,0:T(8,128)S(1)} %convolution_add_fusion.5), channel_id=1, source_target_pairs={{0,4},{4,8},{8,12},{12,16},{16,20},{20,24},{24,28},{1,5},{5,9},{9,... | collective-permute-start | bytes 786440 | tf_op jit(solution)/shard_map/while/body/eval_jaxpr/ppermute | solution.py:15
  170.7 7.7 %collective-permute-start = (f32[4,128,128]{2,1,0:T(8,128)S(1)}, f32[4,128,128]{2,1,0:T(8,128)S(1)}, u32[]{:S(2)}, u32[]{:S(2)}) collective-permute-start(f32[4,128,128]{2,1,0:T(8,128)S(1)} %convolution_add_fusion.5), channel_id=1, source_target_pairs={{0,4},{4,8},{8,12},{12,16},{16,20},{20,24},{24,28},{1,5},{5,9},{9,... | collective-permute-start | bytes 786440 | tf_op jit(solution)/shard_map/while/body/eval_jaxpr/ppermute | solution.py:15
  178.4 1.6 copy-start.2
  181.8 1.0 copy-start.4
  185.1 0.7 copy-start.9
where the time goes:
time: 197 us
  other arithmetic  81 us (41%)
  waiting for transfers between devices  49.1 us (25%)
  starting transfers between devices  32.1 us (16%)
  matrix products  16 us (8%)
  blocking collectives  9.72 us (5%)
  local copies, waits for them, and re-layouts  8.3 us (4%)
    another operation x2, other arithmetic, key_terms(): jax.scipy.linalg.solve_triangular(system, scaled, lower=True, unit_diagon...  78.6 us
    ppermute x7, waiting for transfers between devices, from_behind(): lax.ppermute(value, axis, [(source, source + steps) for source in range(i...  40.3 us
    ppermute x7, starting transfers between devices, from_behind(): lax.ppermute(value, axis, [(source, source + steps) for source in range(i...  13.4 us
    all_to_all x1, blocking collectives, local(): lax.all_to_all(normed, 'head', split_axis=0, concat_axis=1, tiled=True)  9.72 us
    dot_general x15, matrix products, multiply(): return jnp.einsum('...ij,...jk->...ik', left, right, precision=HIGH)  9.32 us
    unnamed x27, local copies, waits for them, and re-layouts  7.03 us
    all_to_all x1, waiting for transfers between devices, local(): lax.all_to_all(keys, 'head', split_axis=1, concat_axis=0, tiled=True)  5.17 us
    all_to_all x1, starting transfers between devices, local(): lax.all_to_all(queries, 'head', split_axis=1, concat_axis=0, tiled=True)  4.17 us
  transfers between devices with their start and end apart: 12, of which 10 were waited for; matrix products, arithmetic and copies ran while one was open for 50% of the time, Pallas kernels for 0%

commit v1 on v0

v1 whole, which is shorter than its diff:
```python
import functools

import jax
import jax.numpy as jnp
from jax import lax
from jax.experimental import pallas as pl
from jax.experimental.pallas import tpu as pltpu
from jax.sharding import PartitionSpec as P

PACK = 4
MESH = pl.DeviceIdType.MESH
F32, BF16 = jnp.float32, jnp.bfloat16


def dot(left, right, dims=((1,), (0,))):
    return lax.dot_general(left, right, (dims, ((), ())), preferred_element_type=F32)


def split(tensor):
    high = tensor.astype(BF16)
    return high, (tensor - high.astype(F32)).astype(BF16)


def dot3(left, right):
    left_high, left_low = split(left)
    right_high, right_low = split(right)
    return dot(left_high, right_high) + (dot(left_low, right_high) + dot(left_high, right_low))


def unit(tensor):
    flat = tensor.astype(F32).reshape(-1, tensor.shape[-1])
    return flat * lax.rsqrt(jnp.sum(flat * flat, axis=-1, keepdims=True) + 1e-06)


def kernel(
    n_seq, n_head, q_ref, k_ref, v_ref, decay_ref, beta_ref, gain_ref, out_ref,
    q_rows, k_rows, v_rows, out_rows, terms_out, terms_in, through, offset,
    maps_high, maps_low, maps_add, chain_in, chain_out, states_out, states_in,
    terms_send, terms_recv, chain_send, chain_recv, states_send, states_recv,
):
    seq, me = lax.axis_index("seq"), lax.axis_index("head")
    tokens, heads, width = q_ref.shape
    own = heads // n_head
    rows = own * tokens

    def partner(step):
        return {"head": lax.rem(me + step, n_head)}

    barrier = pltpu.get_barrier_semaphore()
    for step in range(1, n_head):
        pl.semaphore_signal(barrier, inc=1, device_id=partner(step), device_id_type=MESH)
    for side in (1, n_seq - 1):
        pl.semaphore_signal(
            barrier, inc=1, device_id={"seq": lax.rem(seq + side, n_seq)}, device_id_type=MESH
        )

    k_rows[...] = unit(k_ref[...])
    v_rows[...] = v_ref[...].astype(F32).reshape(-1, width)
    q_rows[...] = unit(q_ref[...]) * width ** (-0.5)

    row_t = lax.broadcasted_iota(jnp.int32, (tokens, tokens), 0)
    col_t = lax.broadcasted_iota(jnp.int32, (tokens, tokens), 1)
    cumulative = dot(jnp.where(row_t >= col_t, 1.0, 0.0).astype(BF16), decay_ref[...])
    betas = beta_ref[...].astype(F32)
    lane = lax.broadcasted_iota(jnp.int32, (tokens, heads), 1)

    size = PACK * tokens
    row = lax.broadcasted_iota(jnp.int32, (size, size), 0)
    col = lax.broadcasted_iota(jnp.int32, (size, size), 1)

    def same(block):
        return (row // block) == (col // block)

    within = same(tokens) & (row >= col)
    strict = same(tokens) & (row > col)
    identity = jnp.where(row == col, 1.0, 0.0)

    def terms_copy(step):
        return pltpu.make_async_remote_copy(
            src_ref=terms_out.at[step], dst_ref=terms_in.at[me],
            send_sem=terms_send.at[step], recv_sem=terms_recv.at[step],
            device_id=partner(step), device_id_type=MESH,
        )

    def pack_terms(units):
        ids = [lax.rem(me + step, n_head) * own + part for step, part in units]

        def stack(ref):
            return jnp.concatenate([ref[pl.ds(i, tokens, stride=heads), :] for i in ids], axis=0)

        def column(gate, i):
            picked = jnp.sum(jnp.where(lane == i, gate, 0.0), axis=1, keepdims=True)
            return jnp.broadcast_to(picked, (tokens, width))

        cums = [column(cumulative, i) for i in ids]
        ends = [jnp.broadcast_to(c[tokens - 1 :, :], (tokens, width)) for c in cums]
        cum = jnp.concatenate(cums, axis=0)
        end = jnp.concatenate(ends, axis=0)
        beta = jnp.concatenate([column(betas, i) for i in ids], axis=0)
        wide = lambda t: jnp.concatenate([t] * (size // width), axis=1)
        across = jnp.transpose(cum)[0:1, :]
        spread = jnp.exp(jnp.where(within, wide(cum) - across, -1e30))
        keys = stack(k_rows).astype(BF16)
        keys_wide = keys.astype(F32)
        lower = jnp.where(strict, dot(keys, keys, ((1,), (1,))) * spread, 0.0) * wide(beta)
        power = jnp.where(same(16), lower, 0.0)
        inverse = identity - power
        for _ in range(3):
            power = dot3(power, power)
            inverse = inverse + dot3(inverse, power)
        block = 16
        while block < tokens:
            corner = jnp.where(same(2 * block) & ~same(block), lower, 0.0)
            inverse = inverse - dot3(dot3(inverse, corner), inverse)
            block *= 2
        grown = jnp.exp(cum)
        right = jnp.concatenate([stack(v_rows) * beta, keys_wide * (grown * beta)], axis=1)
        solved = dot3(inverse, right)
        pseudo, erasers = solved[:, :width].astype(BF16), solved[:, width:].astype(BF16)
        carried = (keys_wide * jnp.exp(end - cum)).astype(BF16)
        decays = [jnp.exp(c[tokens - 1 :, :]) for c in cums]
        return ids, cum, spread, keys, pseudo, erasers, carried, decays, grown

    def store_terms(units, data):
        _, _, _, _, pseudo, erasers, carried, decays, _ = data
        tail_row = lax.broadcasted_iota(jnp.int32, (16, width), 0)
        for at in range(0, PACK, own):
            step = units[at][0]
            tail = jnp.zeros((16, width), F32)
            for part in range(own):
                high, low = split(decays[at + part])
                tail = jnp.where(tail_row == 2 * part, high.astype(F32), tail)
                tail = jnp.where(tail_row == 2 * part + 1, low.astype(F32), tail)
            section = slice(at * tokens, at * tokens + rows)
            target = terms_in.at[me] if step == 0 else terms_out.at[step]
            target[0:rows, :] = pseudo[section]
            target[rows : 2 * rows, :] = erasers[section]
            target[2 * rows : 3 * rows, :] = carried[section]
            target[3 * rows :, :] = tail.astype(BF16)
            if step:
                terms_copy(step).start()

    def query_terms(base, data):
        ids, _, spread, keys, pseudo, erasers, _, _, grown = data
        queries = jnp.concatenate(
            [q_rows[pl.ds(i, tokens, stride=heads), :] for i in ids], axis=0
        ).astype(BF16)
        scores = (dot(queries, keys, ((1,), (1,))) * spread).astype(BF16)
        mixed = dot(scores, jnp.concatenate([pseudo, erasers], axis=1))
        through[base : base + size, :] = (
            queries.astype(F32) * grown - mixed[:, width:]
        ).astype(BF16)
        offset[base : base + size, :] = mixed[:, :width]

    order = list(range(1, n_head)) + [0]
    units = [(step, part) for step in order for part in range(own)]
    packs = [units[at : at + PACK] for at in range(0, len(units), PACK)]
    kept = []
    for at, pack in enumerate(packs):
        data = pack_terms(pack)
        if at == 0:
            pl.semaphore_wait(barrier, n_head + 1)
        store_terms(pack, data)
        kept.append(data)
    for at, data in enumerate(kept):
        query_terms(at * size, data)

    for step in range(1, n_head):
        terms_copy(step).wait_recv()
    eye = jnp.where(
        lax.broadcasted_iota(jnp.int32, (width, width), 0)
        == lax.broadcasted_iota(jnp.int32, (width, width), 1), 1.0, 0.0,
    )
    for part in range(own):
        current = jnp.concatenate([eye, jnp.zeros((width, width), F32)], axis=1)
        for group in range(n_head + 1):
            high, low = split(current[:, :width])
            section = slice(group * width, (group + 1) * width)
            maps_high[part, section, :] = high
            maps_low[part, section, :] = low
            maps_add[part, section, :] = current[:, width:]
            if group == n_head:
                break
            at = part * tokens
            pseudo = terms_in[group, at : at + tokens, :]
            erasers = terms_in[group, rows + at : rows + at + tokens, :]
            carried = terms_in[group, 2 * rows + at : 2 * rows + at + tokens, :]
            tail = terms_in[group, 3 * rows :, :].astype(F32)
            decay = tail[2 * part : 2 * part + 1, :] + tail[2 * part + 1 : 2 * part + 2, :]
            erased = dot(erasers, current.astype(BF16))
            change = jnp.concatenate(
                [erased[:, :width], erased[:, width:] - pseudo.astype(F32)], axis=1
            ).astype(BF16)
            current = current * jnp.concatenate([decay, decay], axis=1) - dot(
                carried, change, ((0,), (0,))
            )

    def chain_copy(part):
        return pltpu.make_async_remote_copy(
            src_ref=chain_out.at[part], dst_ref=chain_in.at[part],
            send_sem=chain_send.at[part], recv_sem=chain_recv.at[part],
            device_id={"seq": lax.rem(seq + 1, n_seq)}, device_id_type=MESH,
        )

    def states_copy(step, part):
        slot = n_head - step
        return pltpu.make_async_remote_copy(
            src_ref=states_out.at[step, part], dst_ref=states_in.at[slot, part],
            send_sem=states_send.at[step, part], recv_sem=states_recv.at[slot, part],
            device_id=partner(step), device_id_type=MESH,
        )

    def mapped(part, group, state):
        section = pl.ds(pl.multiple_of(group * width, width), width)
        high, low = state
        first = maps_high[part, section, :]
        return (
            dot(first, high) + (dot(maps_low[part, section, :], high) + dot(first, low))
        ) + maps_add[part, section, :]

    @pl.when(seq == 0)
    def _():
        chain_in[...] = jnp.zeros_like(chain_in)

    def give_states(part):
        state = split(chain_in[part])
        for step in order:
            entry = mapped(part, lax.rem(me + step, n_head), state).astype(BF16)
            if step:
                states_out[step, part] = entry
                states_copy(step, part).start()
            else:
                states_in[0, part] = entry

    for part in range(own):
        @pl.when(seq > 0)
        def _():
            chain_copy(part).wait_recv()

        chain_out[part] = mapped(part, n_head, split(chain_in[part]))

        @pl.when(seq < n_seq - 1)
        def _():
            chain_copy(part).start()

        if part:
            give_states(part - 1)
    give_states(own - 1)

    gain = gain_ref[...]
    for step in [0] + list(range(n_head - 1, 0, -1)):
        for part in range(own):
            if step:
                states_copy(n_head - step, part).wait_recv()
            at = (order.index(step) * own + part) * tokens
            core = dot(through[at : at + tokens, :], states_in[step, part])
            core = core + offset[at : at + tokens, :]
            scale = lax.rsqrt(jnp.mean(core * core, axis=-1, keepdims=True) + 1e-06)
            head = lax.rem(me + step, n_head) * own + part
            out_rows[pl.ds(head, tokens, stride=heads), :] = core * scale * gain
    out_ref[...] = out_rows[...].reshape(tokens, heads, width).astype(BF16)

    for step in range(1, n_head):
        terms_copy(step).wait_send()
        for part in range(own):
            states_copy(step, part).wait_send()

    @pl.when(seq < n_seq - 1)
    def _():
        for part in range(own):
            chain_copy(part).wait_send()


def solution(mesh):
    n_seq, n_head = mesh.shape["seq"], mesh.shape["head"]

    def local(queries, keys, values, log_decay, beta, norm_gain):
        tokens, heads, width = queries.shape
        own = heads // n_head
        length = tokens * heads
        vmem = pl.BlockSpec(memory_space=pltpu.VMEM)
        payload = (n_head, 3 * own * tokens + 16, width)
        maps = (own, (n_head + 1) * width, width)
        dma = pltpu.SemaphoreType.DMA
        return pl.pallas_call(
            functools.partial(kernel, n_seq, n_head),
            out_shape=jax.ShapeDtypeStruct(queries.shape, BF16),
            in_specs=[vmem] * 6,
            out_specs=vmem,
            scratch_shapes=[
                pltpu.VMEM((length, width), F32),
                pltpu.VMEM((length, width), F32),
                pltpu.VMEM((length, width), F32),
                pltpu.VMEM((length, width), F32),
                pltpu.VMEM(payload, BF16),
                pltpu.VMEM(payload, BF16),
                pltpu.VMEM((length, width), BF16),
                pltpu.VMEM((length, width), F32),
                pltpu.VMEM(maps, BF16),
                pltpu.VMEM(maps, BF16),
                pltpu.VMEM(maps, F32),
                pltpu.VMEM((own, width, width), F32),
                pltpu.VMEM((own, width, width), F32),
                pltpu.VMEM((n_head, own, width, width), BF16),
                pltpu.VMEM((n_head, own, width, width), BF16),
                dma((n_head,)),
                dma((n_head,)),
                dma((own,)),
                dma((own,)),
                dma((n_head, own)),
                dma((n_head, own)),
            ],
            compiler_params=pltpu.CompilerParams(
                collective_id=0, has_side_effects=True, vmem_limit_bytes=48 * 1024 * 1024
            ),
            name="gated_delta",
        )(queries, keys, values, log_decay, beta, norm_gain.reshape(1, width))

    tokens_by_device = P(("seq", "head"), None, None)
    placed = (tokens_by_device,) * 3 + (P(("seq", "head"), None),) * 2 + (P(),)
    return jax.shard_map(
        local, mesh=mesh, in_specs=placed, out_specs=tokens_by_device, check_vma=False
    )
```

time: 197 us -> 48.5 us (0.25)
  the two profiles are of different devices: /device:TPU:24 before, /device:TPU:25 now
where the time goes in v1:
time: 48.5 us; the launch traced here: 48.2 us
  Pallas kernels  43.2 us (89%)
  local copies, waits for them, and re-layouts  5 us (10%)
    pallas_call x1, Pallas kernels, local(): pl.pallas_call(functools.partial(kernel, n_seq, n_head), out_shape=jax.Sh...  43.2 us
    unnamed x13, local copies, waits for them, and re-layouts  5 us

profile of v1, /device:TPU:25, one launch (start us, length us, event | category | flops | bytes accessed | tf_op | source)
XLA Modules:
  0.0 48.2 jit_solution(2993080018938757340)
XLA Ops:
  0.0 0.0 copy-start.4
  0.0 0.8 %copy.7.decay_ref = bf16[64,16]{1,0:T(8,128)(2,1)S(1)} copy(bf16[64,16]{0,1:T(8,128)(2,1)} %param.9) | data formatting | bytes 4096 | tf_op args[3]
  0.8 0.0 copy-done.4
  0.8 0.0 copy-start.3
  0.8 0.1 copy.8.beta_ref
  0.9 0.5 %copy-done.3 = f32[128]{0:T(128)S(1)} copy-done((f32[128]{0:T(128)S(1)}, f32[128]{0:T(128)}, u32[]{:S(2)}) %copy-start.3) | copy-done | bytes 536
  1.5 0.0 copy-start
  1.5 0.9 %copy-done = bf16[64,16,128]{2,1,0:T(8,128)(2,1)S(1)} copy-done((bf16[64,16,128]{2,1,0:T(8,128)(2,1)S(1)}, bf16[64,16,128]{2,1,0:T(8,128)(2,1)}, u32[]{:S(2)}) %copy-start) | copy-done | bytes 262168
  2.4 0.0 copy-start.1
  2.4 0.9 %copy-done.1 = bf16[64,16,128]{2,1,0:T(8,128)(2,1)S(1)} copy-done((bf16[64,16,128]{2,1,0:T(8,128)(2,1)S(1)}, bf16[64,16,128]{2,1,0:T(8,128)(2,1)}, u32[]{:S(2)}) %copy-start.1) | copy-done | bytes 262168
  3.4 0.0 copy-start.2
  3.4 0.9 %copy-done.2 = bf16[64,16,128]{2,1,0:T(8,128)(2,1)S(1)} copy-done((bf16[64,16,128]{2,1,0:T(8,128)(2,1)S(1)}, bf16[64,16,128]{2,1,0:T(8,128)(2,1)}, u32[]{:S(2)}) %copy-start.2) | copy-done | bytes 262168
  4.3 43.2 %gated_delta.1 = bf16[64,16,128]{2,1,0:T(8,128)(2,1)S(1)} custom-call(bf16[64,16,128]{2,1,0:T(8,128)(2,1)S(1)} %copy-done, bf16[64,16,128]{2,1,0:T(8,128)(2,1)S(1)} %copy-done.1, bf16[64,16,128]{2,1,0:T(8,128)(2,1)S(1)} %copy-done.2, bf16[64,16]{1,0:T(8,128)(2,1)S(1)} %copy.7.decay_ref, bf16[64,16]{1,0:T(8,128)(2,1)S(1)} %copy.8.beta_ref, f32[1,128]{1,0:T(1,128)S(1)} %bitcast.1), custom_call_target="tpu_custom_call" | custom-call | tf_op jit(solution)/shard_map/gated_delta/pallas_call | solution.py:285
  47.5 0.7 %copy.10 = bf16[64,16,128]{2,1,0:T(8,128)(2,1)} copy(bf16[64,16,128]{2,1,0:T(8,128)(2,1)S(1)} %gated_delta.1) | data formatting | bytes 524288
Async XLA Ops:
  0.0 0.8 %copy-start.4 = (bf16[64,16]{0,1:T(8,128)(2,1)S(1)}, bf16[64,16]{0,1:T(8,128)(2,1)}, u32[]{:S(2)}) copy-start(bf16[64,16]{0,1:T(8,128)(2,1)} %param.10) | copy-start | bytes 6148
  0.8 0.7 %copy-start.3 = (f32[128]{0:T(128)S(1)}, f32[128]{0:T(128)}, u32[]{:S(2)}) copy-start(f32[128]{0:T(128)} %param.11) | copy-start | bytes 1540
  1.5 0.9 %copy-start = (bf16[64,16,128]{2,1,0:T(8,128)(2,1)S(1)}, bf16[64,16,128]{2,1,0:T(8,128)(2,1)}, u32[]{:S(2)}) copy-start(bf16[64,16,128]{2,1,0:T(8,128)(2,1)} %q_ref.1) | copy-start | bytes 786436
  2.4 0.9 %copy-start.1 = (bf16[64,16,128]{2,1,0:T(8,128)(2,1)S(1)}, bf16[64,16,128]{2,1,0:T(8,128)(2,1)}, u32[]{:S(2)}) copy-start(bf16[64,16,128]{2,1,0:T(8,128)(2,1)} %k_ref.1) | copy-start | bytes 786436
  3.4 0.9 %copy-start.2 = (bf16[64,16,128]{2,1,0:T(8,128)(2,1)S(1)}, bf16[64,16,128]{2,1,0:T(8,128)(2,1)}, u32[]{:S(2)}) copy-start(bf16[64,16,128]{2,1,0:T(8,128)(2,1)} %v_ref.1) | copy-start | bytes 786436

commit v2 on v1

v2 whole, which is shorter than its diff:
```python
import functools

import jax
import jax.numpy as jnp
from jax import lax
from jax.experimental import pallas as pl
from jax.experimental.pallas import tpu as pltpu
from jax.sharding import PartitionSpec as P

PACK = 2
BATCH = 4
MESH = pl.DeviceIdType.MESH
F32, BF16 = jnp.float32, jnp.bfloat16
NT, TN = ((1,), (1,)), ((0,), (0,))


def dot(left, right, dims=((1,), (0,))):
    return lax.dot_general(left, right, (dims, ((), ())), preferred_element_type=F32)


def short(tensors):
    return [tensor.astype(BF16) for tensor in tensors]


def unit(tensor):
    flat = tensor.astype(F32).reshape(-1, tensor.shape[-1])
    return flat * lax.rsqrt(jnp.sum(flat * flat, axis=-1, keepdims=True) + 1e-06)


def kernel(
    n_seq, n_head, q_hbm, k_hbm, v_hbm, decay_hbm, beta_hbm, gain_hbm, out_ref,
    q_ref, k_ref, v_ref, decay_ref, beta_ref, gain_ref,
    q_rows, k_rows, v_rows, row_gate, terms_out, terms_in, query_out, query_in, offset,
    prefix, slab_high, slab_low, slab_add, query_map, query_add,
    chain_in, chain_out, core_out, core_in,
    load_sem, terms_send, terms_recv, query_send, query_recv,
    chain_send, chain_recv, core_send, core_recv,
):
    seq, me = lax.axis_index("seq"), lax.axis_index("head")
    tokens, heads, width = q_ref.shape
    own = heads // n_head
    rows = own * tokens

    def partner(step):
        return {"head": lax.rem(me + step, n_head)}

    sources = (decay_hbm, beta_hbm, k_hbm, v_hbm, q_hbm, gain_hbm)
    targets = (decay_ref, beta_ref, k_ref, v_ref, q_ref, gain_ref)
    loads = [
        pltpu.make_async_copy(source, target, load_sem.at[at])
        for at, (source, target) in enumerate(zip(sources, targets))
    ]
    for load in loads:
        load.start()

    barrier = pltpu.get_barrier_semaphore()
    for step in range(1, n_head):
        pl.semaphore_signal(barrier, inc=1, device_id=partner(step), device_id_type=MESH)
    for side in (1, n_seq - 1):
        pl.semaphore_signal(
            barrier, inc=1, device_id={"seq": lax.rem(seq + side, n_seq)}, device_id_type=MESH
        )

    size = PACK * tokens
    row = lax.broadcasted_iota(jnp.int32, (size, size), 0)
    col = lax.broadcasted_iota(jnp.int32, (size, size), 1)

    def same(block):
        return (row // block) == (col // block)

    within = same(tokens) & (row >= col)
    strict = same(tokens) & (row > col)
    identity = jnp.where(row == col, 1.0, 0.0)
    first_head = lax.broadcasted_iota(jnp.int32, (1, size), 1) < tokens
    row_t = lax.broadcasted_iota(jnp.int32, (tokens, tokens), 0)
    col_t = lax.broadcasted_iota(jnp.int32, (tokens, tokens), 1)
    token_of = lax.rem(lax.broadcasted_iota(jnp.int32, (tokens, size), 1), tokens)
    before = lax.broadcasted_iota(jnp.int32, (tokens, size), 0) <= token_of
    lane = lax.broadcasted_iota(jnp.int32, (tokens, heads), 1)

    loads[0].wait()
    row_gate[...] = dot(decay_ref[...], jnp.where(before, 1.0, 0.0).astype(BF16))
    cumulative = dot(jnp.where(row_t >= col_t, 1.0, 0.0).astype(BF16), decay_ref[...], NT)
    loads[1].wait()
    betas = dot(jnp.where(row_t == col_t, 1.0, 0.0).astype(BF16), beta_ref[...], NT)
    loads[2].wait()
    k_rows[...] = unit(k_ref[...])
    loads[3].wait()
    v_rows[...] = v_ref[...].astype(F32).reshape(-1, width)
    loads[4].wait()
    q_rows[...] = unit(q_ref[...]) * width ** (-0.5)
    loads[5].wait()

    def stack(ref, ids):
        return jnp.concatenate([ref[pl.ds(i, tokens, stride=heads), :] for i in ids], axis=0)

    def column(gate, i):
        picked = jnp.sum(jnp.where(lane == i, gate, 0.0), axis=1, keepdims=True)
        return jnp.broadcast_to(picked, (tokens, width))

    def batch_terms(packs):
        ids = [[lax.rem(me + step, n_head) * own + part for step, part in pack] for pack in packs]
        cums = [[column(cumulative, i) for i in pack] for pack in ids]
        ends = [[c[tokens - 1 :, :] for c in pack] for pack in cums]
        cum = [jnp.concatenate(pack, axis=0) for pack in cums]
        end = [
            jnp.concatenate([jnp.broadcast_to(e, (tokens, width)) for e in pack], axis=0)
            for pack in ends
        ]
        beta = [jnp.concatenate([column(betas, i) for i in pack], axis=0) for pack in ids]
        across = [
            jnp.where(first_head, row_gate[pl.ds(pack[0], 1), :], row_gate[pl.ds(pack[1], 1), :])
            for pack in ids
        ]
        spread = [jnp.exp(jnp.where(within, c - a, -1e30)) for c, a in zip(cum, across)]
        keys = [stack(k_rows, pack).astype(BF16) for pack in ids]
        lower = [
            jnp.where(strict, dot(k, k, NT) * s, 0.0) * b for k, s, b in zip(keys, spread, beta)
        ]
        block = 8
        inner = [jnp.where(same(block), a, 0.0) for a in lower]
        inner_short = short(inner)
        inverse = [identity - a for a in inner]
        square = short([dot(a, a) for a in inner_short])
        fourth = short([dot(a, a) for a in square])
        inverse = [x + dot(y, a) for x, y, a in zip(inverse, short(inverse), square)]
        inverse = [x + dot(y, a) for x, y, a in zip(inverse, short(inverse), fourth)]
        grown = [jnp.exp(c) for c in cum]
        wide = [k.astype(F32) for k in keys]
        right = short([
            jnp.concatenate([stack(v_rows, pack) * b, w * (g * b)], axis=1)
            for pack, b, w, g in zip(ids, beta, wide, grown)
        ])
        while block < tokens:
            between = same(2 * block) & ~same(block)
            corner = short([jnp.where(between, a, 0.0) for a in lower])
            held = short(inverse)
            crossed = short([dot(x, a) for x, a in zip(held, corner)])
            block *= 2
            if block < tokens:
                inverse = [x - dot(a, y) for x, a, y in zip(inverse, crossed, held)]
        partly = [dot(x, r) for x, r in zip(held, right)]
        solved = short([y - dot(a, z) for y, a, z in zip(partly, crossed, short(partly))])
        carried = short([w * jnp.exp(e - c) for w, e, c in zip(wide, end, cum)])
        decays = [[jnp.exp(e) for e in pack] for pack in ends]
        return [
            dict(units=pack, ids=i, spread=s, keys=k, solved=x, carried=c, decays=d, grown=g)
            for pack, i, s, k, x, c, d, g in zip(
                packs, ids, spread, keys, solved, carried, decays, grown
            )
        ]

    def terms_copy(step):
        return pltpu.make_async_remote_copy(
            src_ref=terms_out.at[step], dst_ref=terms_in.at[me],
            send_sem=terms_send.at[step], recv_sem=terms_recv.at[step],
            device_id=partner(step), device_id_type=MESH,
        )

    def query_copy(step):
        return pltpu.make_async_remote_copy(
            src_ref=query_out.at[step], dst_ref=query_in.at[me],
            send_sem=query_send.at[step], recv_sem=query_recv.at[step],
            device_id=partner(step), device_id_type=MESH,
        )

    tail_row = lax.broadcasted_iota(jnp.int32, (16, width), 0)

    def store_terms(batch):
        by_step = {}
        for data in batch:
            for at, (step, part) in enumerate(data["units"]):
                target = terms_in.at[me] if step == 0 else terms_out.at[step]
                section, to = slice(at * tokens, (at + 1) * tokens), part * tokens
                target[to : to + tokens, :] = data["solved"][section, :width]
                target[rows + to : rows + to + tokens, :] = data["solved"][section, width:]
                target[2 * rows + to : 2 * rows + to + tokens, :] = data["carried"][section]
                tail = by_step.get(step, jnp.zeros((16, width), F32))
                decay = data["decays"][at]
                high = decay.astype(BF16).astype(F32)
                tail = jnp.where(tail_row == 2 * part, high, tail)
                by_step[step] = jnp.where(tail_row == 2 * part + 1, decay - high, tail)
        for step, tail in by_step.items():
            target = terms_in.at[me] if step == 0 else terms_out.at[step]
            target[3 * rows :, :] = tail.astype(BF16)
            if step:
                terms_copy(step).start()

    def query_terms(batch):
        queries = [stack(q_rows, data["ids"]).astype(BF16) for data in batch]
        scores = short([dot(q, d["keys"], NT) * d["spread"] for q, d in zip(queries, batch)])
        mixed = [dot(s, d["solved"]) for s, d in zip(scores, batch)]
        for q, m, d in zip(queries, mixed, batch):
            through = (q.astype(F32) * d["grown"] - m[:, width:]).astype(BF16)
            for at, (step, part) in enumerate(d["units"]):
                section, to = slice(at * tokens, (at + 1) * tokens), part * tokens
                target = query_in.at[me] if step == 0 else query_out.at[step]
                target[to : to + tokens, :] = through[section]
                offset[step, part] = m[section, :width]

    order = list(range(1, n_head)) + [0]
    units = [(step, part) for step in order for part in range(own)]
    packs = [units[at : at + PACK] for at in range(0, len(units), PACK)]
    kept = []
    for at in range(0, len(packs), BATCH):
        batch = batch_terms(packs[at : at + BATCH])
        if at == 0:
            pl.semaphore_wait(barrier, n_head + 1)
        store_terms(batch)
        kept.append(batch)
    for batch in kept:
        query_terms(batch)
    for step in range(1, n_head):
        query_copy(step).start()

    for step in range(1, n_head):
        terms_copy(step).wait_recv()
    eye = jnp.where(
        lax.broadcasted_iota(jnp.int32, (width, width), 0)
        == lax.broadcasted_iota(jnp.int32, (width, width), 1), 1.0, 0.0,
    )
    current = [jnp.concatenate([eye, jnp.zeros((width, width), F32)], axis=1)] * own
    for group in range(n_head):
        tail = terms_in[group, 3 * rows :, :].astype(F32)
        held = short(current)
        for part in range(own):
            prefix[part, group] = held[part]
        for part in range(own):
            at = part * tokens
            pseudo = terms_in[group, at : at + tokens, :]
            erasers = terms_in[group, rows + at : rows + at + tokens, :]
            carried = terms_in[group, 2 * rows + at : 2 * rows + at + tokens, :]
            decay = tail[2 * part : 2 * part + 1, :] + tail[2 * part + 1 : 2 * part + 2, :]
            if group:
                erased = dot(erasers, held[part])
                change = jnp.concatenate(
                    [erased[:, :width], erased[:, width:] - pseudo.astype(F32)], axis=1
                ).astype(BF16)
            else:
                change = jnp.concatenate([erasers, -pseudo], axis=1)
            decay = jnp.concatenate([decay, decay], axis=1)
            current[part] = current[part] * decay - dot(carried, change, TN)
    for part in range(own):
        high = current[part][:, :width].astype(BF16)
        slab_high[part] = high
        slab_low[part] = (current[part][:, :width] - high.astype(F32)).astype(BF16)
        slab_add[part] = current[part][:, width:]

    def chain_copy(part):
        return pltpu.make_async_remote_copy(
            src_ref=chain_out.at[part], dst_ref=chain_in.at[part],
            send_sem=chain_send.at[part], recv_sem=chain_recv.at[part],
            device_id={"seq": lax.rem(seq + 1, n_seq)}, device_id_type=MESH,
        )

    def core_copy(step, part):
        slot = n_head - step
        group = lax.rem(me + step, n_head)
        return pltpu.make_async_remote_copy(
            src_ref=core_out.at[part, group], dst_ref=core_in.at[slot, part],
            send_sem=core_send.at[step, part], recv_sem=core_recv.at[slot, part],
            device_id=partner(step), device_id_type=MESH,
        )

    def map_queries():
        for step in range(1, n_head):
            query_copy(step).wait_recv()
        for group in range(n_head):
            for part in range(own):
                section = slice(group * tokens, (group + 1) * tokens)
                at = part * tokens
                queries = query_in[group, at : at + tokens, :]
                mapped = dot(queries, prefix[part, group])
                query_map[part, section, :] = mapped[:, :width].astype(BF16)
                query_add[part, section, :] = mapped[:, width:]

    def pass_on(part):
        @pl.when(seq > 0)
        def _():
            chain_copy(part).wait_recv()

        @pl.when(seq < n_seq - 1)
        def _():
            state = chain_in[part]
            moved = dot(slab_high[part], state) + dot(slab_low[part], state)
            chain_out[part] = (moved + slab_add[part]).astype(BF16)
            chain_copy(part).start()

    def give_cores(part):
        cores = dot(query_map[part], chain_in[part]) + query_add[part]
        core_out[part] = cores.astype(BF16).reshape(n_head, tokens, width)
        for step in range(1, n_head):
            core_copy(step, part).start()

    @pl.when(seq == 0)
    def _():
        chain_in[...] = jnp.zeros_like(chain_in)

    late = seq >= n_seq // 2

    @pl.when(late)
    def _():
        map_queries()
        for part in range(own):
            pass_on(part)
            give_cores(part)

    @pl.when(jnp.logical_not(late))
    def _():
        for part in range(own):
            pass_on(part)
        map_queries()
        for part in range(own):
            give_cores(part)

    gain = gain_ref[...]
    for step in [0] + list(range(n_head - 1, 0, -1)):
        for part in range(own):
            if step:
                core_copy(n_head - step, part).wait_recv()
                core = core_in[step, part]
            else:
                core = core_out[part, me]
            core = core.astype(F32) + offset[step, part]
            scale = lax.rsqrt(jnp.mean(core * core, axis=-1, keepdims=True) + 1e-06)
            head = lax.rem(me + step, n_head) * own + part
            out_ref[pl.ds(head, tokens, stride=heads), :] = core * scale * gain

    for step in range(1, n_head):
        terms_copy(step).wait_send()
        query_copy(step).wait_send()
        for part in range(own):
            core_copy(step, part).wait_send()

    @pl.when(seq < n_seq - 1)
    def _():
        for part in range(own):
            chain_copy(part).wait_send()


def solution(mesh):
    n_seq, n_head = mesh.shape["seq"], mesh.shape["head"]

    def local(queries, keys, values, log_decay, beta, norm_gain):
        tokens, heads, width = queries.shape
        own = heads // n_head
        length = tokens * heads
        hbm = pl.BlockSpec(memory_space=pltpu.HBM)
        payload = (n_head, 3 * own * tokens + 16, width)
        dma = pltpu.SemaphoreType.DMA
        rows = pl.pallas_call(
            functools.partial(kernel, n_seq, n_head),
            out_shape=jax.ShapeDtypeStruct((length, width), F32),
            in_specs=[hbm] * 6,
            out_specs=pl.BlockSpec(memory_space=pltpu.VMEM),
            scratch_shapes=[
                pltpu.VMEM(queries.shape, BF16),
                pltpu.VMEM(queries.shape, BF16),
                pltpu.VMEM(queries.shape, BF16),
                pltpu.VMEM((heads, tokens), BF16),
                pltpu.VMEM((heads, tokens), BF16),
                pltpu.VMEM((1, width), F32),
                pltpu.VMEM((length, width), F32),
                pltpu.VMEM((length, width), F32),
                pltpu.VMEM((length, width), F32),
                pltpu.VMEM((heads, PACK * tokens), F32),
                pltpu.VMEM(payload, BF16),
                pltpu.VMEM(payload, BF16),
                pltpu.VMEM((n_head, own * tokens, width), BF16),
                pltpu.VMEM((n_head, own * tokens, width), BF16),
                pltpu.VMEM((n_head, own, tokens, width), F32),
                pltpu.VMEM((own, n_head, width, 2 * width), BF16),
                pltpu.VMEM((own, width, width), BF16),
                pltpu.VMEM((own, width, width), BF16),
                pltpu.VMEM((own, width, width), F32),
                pltpu.VMEM((own, n_head * tokens, width), BF16),
                pltpu.VMEM((own, n_head * tokens, width), F32),
                pltpu.VMEM((own, width, width), BF16),
                pltpu.VMEM((own, width, width), BF16),
                pltpu.VMEM((own, n_head, tokens, width), BF16),
                pltpu.VMEM((n_head, own, tokens, width), BF16),
                dma((6,)),
                dma((n_head,)),
                dma((n_head,)),
                dma((n_head,)),
                dma((n_head,)),
                dma((own,)),
                dma((own,)),
                dma((n_head, own)),
                dma((n_head, own)),
            ],
            compiler_params=pltpu.CompilerParams(
                collective_id=0, has_side_effects=True, vmem_limit_bytes=63 * 1024 * 1024
            ),
            name="gated_delta",
        )(queries, keys, values, log_decay.T, beta.T, norm_gain.reshape(1, width))
        return rows.reshape(tokens, heads, width).astype(BF16)

    tokens_by_device = P(("seq", "head"), None, None)
    placed = (tokens_by_device,) * 3 + (P(("seq", "head"), None),) * 2 + (P(),)
    return jax.shard_map(
        local, mesh=mesh, in_specs=placed, out_specs=tokens_by_device, check_vma=False
    )
```

time: 48.5 us -> 37.1 us (0.76)
  Pallas kernels: 43.2 us -> 35.1 us
  local copies, waits for them, and re-layouts: 5 us -> 0 us
  other arithmetic: 0 us -> 1.77 us
    pallas_call x1, Pallas kernels: 43.2 us -> 35.1 us  [local(): pl.pallas_call(functools.partial(kernel, n_seq, n_head), out_shape=jax.Sh...]
    unnamed x13 -> x0, local copies, waits for them, and re-layouts: 5 us -> none
    convert_element_type x0 -> x1, other arithmetic: none -> 1.77 us  [local(): return rows.reshape(tokens, heads, width).astype(BF16)]
where the time goes in v2:
time: 37.1 us; the launch traced here: 36.9 us
  Pallas kernels  35.1 us (95%)
  other arithmetic  1.77 us (5%)
    pallas_call x1, Pallas kernels, local(): pl.pallas_call(functools.partial(kernel, n_seq, n_head), out_shape=jax.Sh...  35.1 us
    convert_element_type x1, other arithmetic, local(): return rows.reshape(tokens, heads, width).astype(BF16)  1.77 us

profile of v2, /device:TPU:25, one launch (start us, length us, event | category | flops | bytes accessed | tf_op | source)
XLA Modules:
  0.0 36.9 jit_solution(3614054655355719841)
XLA Ops:
  0.0 35.1 %gated_delta.1 = f32[1024,128]{1,0:T(8,128)} custom-call(bf16[64,16,128]{2,1,0:T(8,128)(2,1)} %q_hbm.1, bf16[64,16,128]{2,1,0:T(8,128)(2,1)} %k_hbm.1, bf16[64,16,128]{2,1,0:T(8,128)(2,1)} %v_hbm.1, bf16[16,64]{1,0:T(8,128)(2,1)} %bitcast.4, bf16[16,64]{1,0:T(8,128)(2,1)} %bitcast.5, f32[1,128]{1,0:T(1,128)} %bitcast.6), custom_call_target="tpu_custom_call" | custom-call | tf_op jit(solution)/shard_map/gated_delta/pallas_call | solution.py:351
  35.2 1.8 %convert_element_type.6 = bf16[1024,128]{1,0:T(8,128)(2,1)} convert(f32[1024,128]{1,0:T(8,128)} %gated_delta.1) | non-fusion elementwise | flops 131072 | bytes 786432 | tf_op jit(solution)/shard_map/convert_element_type | solution.py:397

commit v3 on v2

--- a/solution.py
+++ b/solution.py
@@ -8,7 +8,7 @@
 from jax.sharding import PartitionSpec as P
 
 PACK = 2
-BATCH = 4
+BATCH = 8
 MESH = pl.DeviceIdType.MESH
 F32, BF16 = jnp.float32, jnp.bfloat16
 NT, TN = ((1,), (1,)), ((0,), (0,))
@@ -30,10 +30,10 @@
 def kernel(
     n_seq, n_head, q_hbm, k_hbm, v_hbm, decay_hbm, beta_hbm, gain_hbm, out_ref,
     q_ref, k_ref, v_ref, decay_ref, beta_ref, gain_ref,
-    q_rows, k_rows, v_rows, row_gate, terms_out, terms_in, query_out, query_in, offset,
+    q_rows, k_rows, v_rows, out_rows, row_gate, beta_rows, kept_gate, terms_out, terms_in, solver_out, solver_in, query_out, query_in, offset,
     prefix, slab_high, slab_low, slab_add, query_map, query_add,
     chain_in, chain_out, core_out, core_in,
-    load_sem, terms_send, terms_recv, query_send, query_recv,
+    load_sem, terms_send, terms_recv, solver_send, solver_recv, query_send, query_recv,
     chain_send, chain_recv, core_send, core_recv,
 ):
     seq, me = lax.axis_index("seq"), lax.axis_index("head")
@@ -79,18 +79,22 @@
     lane = lax.broadcasted_iota(jnp.int32, (tokens, heads), 1)
 
     loads[0].wait()
-    row_gate[...] = dot(decay_ref[...], jnp.where(before, 1.0, 0.0).astype(BF16))
+    log_rows = dot(decay_ref[...], jnp.where(before, 1.0, 0.0).astype(BF16))
+    row_gate[...] = log_rows
+    log_end = log_rows[:, size - 1 :]
+    first_half = lax.broadcasted_iota(jnp.int32, (heads, size), 1) < tokens
+    kept_gate[0] = jnp.exp(jnp.where(first_half, log_rows, log_end - log_rows))
+    kept_gate[1] = jnp.broadcast_to(jnp.exp(log_end), (heads, size))
     cumulative = dot(jnp.where(row_t >= col_t, 1.0, 0.0).astype(BF16), decay_ref[...], NT)
     loads[1].wait()
+    row_beta = dot(beta_ref[...], jnp.where(token_of == lax.broadcasted_iota(
+        jnp.int32, (tokens, size), 0), 1.0, 0.0).astype(BF16))
+    beta_rows[...] = row_beta
     betas = dot(jnp.where(row_t == col_t, 1.0, 0.0).astype(BF16), beta_ref[...], NT)
     loads[2].wait()
     k_rows[...] = unit(k_ref[...])
     loads[3].wait()
     v_rows[...] = v_ref[...].astype(F32).reshape(-1, width)
-    loads[4].wait()
-    q_rows[...] = unit(q_ref[...]) * width ** (-0.5)
-    loads[5].wait()
-
     def stack(ref, ids):
         return jnp.concatenate([ref[pl.ds(i, tokens, stride=heads), :] for i in ids], axis=0)
 
@@ -101,12 +105,7 @@
     def batch_terms(packs):
         ids = [[lax.rem(me + step, n_head) * own + part for step, part in pack] for pack in packs]
         cums = [[column(cumulative, i) for i in pack] for pack in ids]
-        ends = [[c[tokens - 1 :, :] for c in pack] for pack in cums]
         cum = [jnp.concatenate(pack, axis=0) for pack in cums]
-        end = [
-            jnp.concatenate([jnp.broadcast_to(e, (tokens, width)) for e in pack], axis=0)
-            for pack in ends
-        ]
         beta = [jnp.concatenate([column(betas, i) for i in pack], axis=0) for pack in ids]
         across = [
             jnp.where(first_head, row_gate[pl.ds(pack[0], 1), :], row_gate[pl.ds(pack[1], 1), :])
@@ -141,13 +140,16 @@
                 inverse = [x - dot(a, y) for x, a, y in zip(inverse, crossed, held)]
         partly = [dot(x, r) for x, r in zip(held, right)]
         solved = short([y - dot(a, z) for y, a, z in zip(partly, crossed, short(partly))])
-        carried = short([w * jnp.exp(e - c) for w, e, c in zip(wide, end, cum)])
-        decays = [[jnp.exp(e) for e in pack] for pack in ends]
+        scales = [
+            jnp.where(first_head, beta_rows[pl.ds(pack[0], 1), :], beta_rows[pl.ds(pack[1], 1), :])
+            for pack in ids
+        ]
+        solver = [
+            (x - dot(a, y)) * b for x, a, y, b in zip(inverse, crossed, held, scales)
+        ]
         return [
-            dict(units=pack, ids=i, spread=s, keys=k, solved=x, carried=c, decays=d, grown=g)
-            for pack, i, s, k, x, c, d, g in zip(
-                packs, ids, spread, keys, solved, carried, decays, grown
-            )
+            dict(units=pack, ids=i, spread=s, keys=k, solved=x, grown=g, solver=t)
+            for pack, i, s, k, x, g, t in zip(packs, ids, spread, keys, solved, grown, solver)
         ]
 
     def terms_copy(step):
@@ -164,27 +166,47 @@
             device_id=partner(step), device_id_type=MESH,
         )
 
+    def solver_copy(step):
+        return pltpu.make_async_remote_copy(
+            src_ref=solver_out.at[step], dst_ref=solver_in.at[me],
+            send_sem=solver_send.at[step], recv_sem=solver_recv.at[step],
+            device_id=partner(step), device_id_type=MESH,
+        )
+
     tail_row = lax.broadcasted_iota(jnp.int32, (16, width), 0)
 
-    def store_terms(batch):
-        by_step = {}
+    def store_terms(step):
+        target = terms_in.at[me] if step == 0 else terms_out.at[step]
+        tail = jnp.zeros((16, width), F32)
+        for part in range(own):
+            head, to = lax.rem(me + step, n_head) * own + part, part * tokens
+            from_head = pl.ds(head, tokens, stride=heads)
+            target[to : to + tokens, :] = k_rows[from_head, :].astype(BF16)
+            target[rows + to : rows + to + tokens, :] = v_rows[from_head, :].astype(BF16)
+            decay = kept_gate[1, pl.ds(head, 1), :]
+            high = decay.astype(BF16).astype(F32)
+            tail = jnp.where(tail_row == 3 * part, kept_gate[0, pl.ds(head, 1), :], tail)
+            tail = jnp.where(tail_row == 3 * part + 1, high, tail)
+            tail = jnp.where(tail_row == 3 * part + 2, decay - high, tail)
+        target[2 * rows :, :] = tail.astype(BF16)
+        if step:
+            terms_copy(step).start()
+
+    pairs = max(own // 2, 1)
+
+    def store_solvers(batch):
         for data in batch:
+            scaled = data["solver"]
+            top, low = scaled[:tokens], scaled[tokens:]
             for at, (step, part) in enumerate(data["units"]):
-                target = terms_in.at[me] if step == 0 else terms_out.at[step]
-                section, to = slice(at * tokens, (at + 1) * tokens), part * tokens
-                target[to : to + tokens, :] = data["solved"][section, :width]
-                target[rows + to : rows + to + tokens, :] = data["solved"][section, width:]
-                target[2 * rows + to : 2 * rows + to + tokens, :] = data["carried"][section]
-                tail = by_step.get(step, jnp.zeros((16, width), F32))
-                decay = data["decays"][at]
-                high = decay.astype(BF16).astype(F32)
-                tail = jnp.where(tail_row == 2 * part, high, tail)
-                by_step[step] = jnp.where(tail_row == 2 * part + 1, decay - high, tail)
-        for step, tail in by_step.items():
-            target = terms_in.at[me] if step == 0 else terms_out.at[step]
-            target[3 * rows :, :] = tail.astype(BF16)
-            if step:
-                terms_copy(step).start()
+                target = solver_in.at[me] if step == 0 else solver_out.at[step]
+                if own == 1:
+                    mine = (top, low)[at]
+                    both = jnp.concatenate([mine[:, tokens:], mine[:, :tokens]], axis=1) + mine
+                    target[...] = both.astype(BF16)
+                elif at == 0:
+                    to = part // 2 * tokens
+                    target[to : to + tokens, :] = (top + low).astype(BF16)
 
     def query_terms(batch):
         queries = [stack(q_rows, data["ids"]).astype(BF16) for data in batch]
@@ -201,13 +223,19 @@
     order = list(range(1, n_head)) + [0]
     units = [(step, part) for step in order for part in range(own)]
     packs = [units[at : at + PACK] for at in range(0, len(units), PACK)]
+    pl.semaphore_wait(barrier, n_head + 1)
+    for step in order:
+        store_terms(step)
+    loads[4].wait()
+    q_rows[...] = unit(q_ref[...]) * width ** (-0.5)
+    loads[5].wait()
     kept = []
     for at in range(0, len(packs), BATCH):
         batch = batch_terms(packs[at : at + BATCH])
-        if at == 0:
-            pl.semaphore_wait(barrier, n_head + 1)
-        store_terms(batch)
+        store_solvers(batch)
         kept.append(batch)
+    for step in range(1, n_head):
+        solver_copy(step).start()
     for batch in kept:
         query_terms(batch)
     for step in range(1, n_head):
@@ -215,22 +243,55 @@
 
     for step in range(1, n_head):
         terms_copy(step).wait_recv()
+    low_lane = lax.broadcasted_iota(jnp.int32, (tokens, size), 1) < tokens
+    eye_t = row_t == col_t
+    shrunk = []
+    for group in range(n_head):
+        tail = terms_in[group, 2 * rows :, :].astype(F32)
+        for part in range(own):
+            keys = terms_in[group, part * tokens : (part + 1) * tokens, :]
+            shrink = tail[3 * part : 3 * part + 1, tokens:]
+            shrunk.append(dot(jnp.where(eye_t, shrink, 0.0).astype(BF16), keys).astype(BF16))
+    for step in range(1, n_head):
+        solver_copy(step).wait_recv()
+    erasers_of, pseudo_of = [], []
+    for group in range(n_head):
+        tail = terms_in[group, 2 * rows :, :].astype(F32)
+        for pair in range(pairs):
+            solver = solver_in[group, pair * tokens : (pair + 1) * tokens, :].astype(F32)
+            many = min(own, 2)
+            grows = [tail[3 * part : 3 * part + 1, :] for part in range(many * pair, many * pair + many)]
+            if many == 2:
+                mirrored = jnp.concatenate([grows[1][:, tokens:], grows[1][:, :tokens]], axis=1)
+                grow = jnp.where(first_head, grows[0], mirrored)
+                diagonal = lambda t: jnp.concatenate(
+                    [jnp.where(low_lane, t, 0.0), jnp.where(low_lane, 0.0, t)], axis=0
+                ).astype(BF16)
+            else:
+                grow = grows[0]
+                diagonal = lambda t: t[:, :tokens].astype(BF16)
+            section = slice(pair * many * tokens, (pair + 1) * many * tokens)
+            beyond = slice(rows + section.start, rows + section.stop)
+            erasers = dot(diagonal(solver * grow), terms_in[group, section, :]).astype(BF16)
+            pseudo = dot(diagonal(solver), terms_in[group, beyond, :]).astype(BF16)
+            for at in range(many):
+                erasers_of.append(erasers[at * tokens : (at + 1) * tokens])
+                pseudo_of.append(pseudo[at * tokens : (at + 1) * tokens])
     eye = jnp.where(
         lax.broadcasted_iota(jnp.int32, (width, width), 0)
         == lax.broadcasted_iota(jnp.int32, (width, width), 1), 1.0, 0.0,
     )
     current = [jnp.concatenate([eye, jnp.zeros((width, width), F32)], axis=1)] * own
     for group in range(n_head):
-        tail = terms_in[group, 3 * rows :, :].astype(F32)
+        tail = terms_in[group, 2 * rows :, :].astype(F32)
         held = short(current)
         for part in range(own):
             prefix[part, group] = held[part]
         for part in range(own):
-            at = part * tokens
-            pseudo = terms_in[group, at : at + tokens, :]
-            erasers = terms_in[group, rows + at : rows + at + tokens, :]
-            carried = terms_in[group, 2 * rows + at : 2 * rows + at + tokens, :]
-            decay = tail[2 * part : 2 * part + 1, :] + tail[2 * part + 1 : 2 * part + 2, :]
+            pseudo = pseudo_of[group * own + part]
+            erasers = erasers_of[group * own + part]
+            carried = shrunk[group * own + part]
+            decay = tail[3 * part + 1 : 3 * part + 2, :] + tail[3 * part + 2 : 3 * part + 3, :]
             if group:
                 erased = dot(erasers, held[part])
                 change = jnp.concatenate(
@@ -324,10 +385,12 @@
             core = core.astype(F32) + offset[step, part]
             scale = lax.rsqrt(jnp.mean(core * core, axis=-1, keepdims=True) + 1e-06)
             head = lax.rem(me + step, n_head) * own + part
-            out_ref[pl.ds(head, tokens, stride=heads), :] = core * scale * gain
+            out_rows[pl.ds(head, tokens, stride=heads), :] = core * scale * gain
+    out_ref[...] = out_rows[...].reshape(tokens, heads, width).astype(BF16)
 
     for step in range(1, n_head):
         terms_copy(step).wait_send()
+        solver_copy(step).wait_send()
         query_copy(step).wait_send()
         for part in range(own):
             core_copy(step, part).wait_send()
@@ -346,11 +409,12 @@
         own = heads // n_head
         length = tokens * heads
         hbm = pl.BlockSpec(memory_space=pltpu.HBM)
-        payload = (n_head, 3 * own * tokens + 16, width)
+        payload = (n_head, 2 * own * tokens + 16, width)
+        solvers = (n_head, max(own // 2, 1) * tokens, 2 * tokens)
         dma = pltpu.SemaphoreType.DMA
-        rows = pl.pallas_call(
+        return pl.pallas_call(
             functools.partial(kernel, n_seq, n_head),
-            out_shape=jax.ShapeDtypeStruct((length, width), F32),
+            out_shape=pltpu.VMEM(queries.shape, BF16),
             in_specs=[hbm] * 6,
             out_specs=pl.BlockSpec(memory_space=pltpu.VMEM),
             scratch_shapes=[
@@ -363,9 +427,14 @@
                 pltpu.VMEM((length, width), F32),
                 pltpu.VMEM((length, width), F32),
                 pltpu.VMEM((length, width), F32),
+                pltpu.VMEM((length, width), F32),
                 pltpu.VMEM((heads, PACK * tokens), F32),
+                pltpu.VMEM((heads, PACK * tokens), F32),
+                pltpu.VMEM((2, heads, PACK * tokens), F32),
                 pltpu.VMEM(payload, BF16),
                 pltpu.VMEM(payload, BF16),
+                pltpu.VMEM(solvers, BF16),
+                pltpu.VMEM(solvers, BF16),
                 pltpu.VMEM((n_head, own * tokens, width), BF16),
                 pltpu.VMEM((n_head, own * tokens, width), BF16),
                 pltpu.VMEM((n_head, own, tokens, width), F32),
@@ -384,17 +453,21 @@
                 dma((n_head,)),
                 dma((n_head,)),
                 dma((n_head,)),
+                dma((n_head,)),
+                dma((n_head,)),
                 dma((own,)),
                 dma((own,)),
                 dma((n_head, own)),
                 dma((n_head, own)),
             ],
             compiler_params=pltpu.CompilerParams(
-                collective_id=0, has_side_effects=True, vmem_limit_bytes=63 * 1024 * 1024
+                collective_id=0, has_side_effects=True, vmem_limit_bytes=48 * 1024 * 1024
             ),
             name="gated_delta",
-        )(queries, keys, values, log_decay.T, beta.T, norm_gain.reshape(1, width))
-        return rows.reshape(tokens, heads, width).astype(BF16)
+        )(*[
+            pltpu.with_memory_space_constraint(array, pltpu.HBM)
+            for array in (queries, keys, values, log_decay.T, beta.T, norm_gain.reshape(1, width))
+        ])
 
     tokens_by_device = P(("seq", "head"), None, None)
     placed = (tokens_by_device,) * 3 + (P(("seq", "head"), None),) * 2 + (P(),)

time: 37.1 us -> 32.6 us (0.88)
  Pallas kernels: 35.1 us -> 31.7 us
  other arithmetic: 1.77 us -> 0 us
  local copies, waits for them, and re-layouts: 0 us -> 0.71 us
    pallas_call x1, Pallas kernels: 35.1 us -> 31.7 us  [local(): pl.pallas_call(functools.partial(kernel, n_seq, n_head), out_shape=pltpu....]
    convert_element_type x1 -> x0, other arithmetic: 1.77 us -> none  [local(): return rows.reshape(tokens, heads, width).astype(BF16)]
    unnamed x0 -> x1, local copies, waits for them, and re-layouts: none -> 0.71 us
where the time goes in v3:
time: 32.6 us; the launch traced here: 32.4 us
  Pallas kernels  31.7 us (97%)
  local copies, waits for them, and re-layouts  0.71 us (2%)
    pallas_call x1, Pallas kernels, local(): pl.pallas_call(functools.partial(kernel, n_seq, n_head), out_shape=pltpu....  31.7 us
    unnamed x1, local copies, waits for them, and re-layouts  0.71 us

profile of v3, /device:TPU:25, one launch (start us, length us, event | category | flops | bytes accessed | tf_op | source)
XLA Modules:
  0.0 32.4 jit_solution(13825103820444999157)
XLA Ops:
  0.0 31.7 %gated_delta.1 = bf16[64,16,128]{2,1,0:T(8,128)(2,1)S(1)} custom-call(bf16[64,16,128]{2,1,0:T(8,128)(2,1)} %q_hbm.1, bf16[64,16,128]{2,1,0:T(8,128)(2,1)} %k_hbm.1, bf16[64,16,128]{2,1,0:T(8,128)(2,1)} %v_hbm.1, bf16[16,64]{1,0:T(8,128)(2,1)} %bitcast.3, bf16[16,64]{1,0:T(8,128)(2,1)} %bitcast.4, f32[1,128]{1,0:T(1,128)} %bitcast.5), custom_call_target="tpu_custom_call" | custom-call | tf_op jit(solution)/shard_map/gated_delta/pallas_call | solution.py:415
  31.7 0.7 %copy.8 = bf16[64,16,128]{2,1,0:T(8,128)(2,1)} copy(bf16[64,16,128]{2,1,0:T(8,128)(2,1)S(1)} %gated_delta.1) | data formatting | bytes 524288

commit v4 on v3

--- a/solution.py
+++ b/solution.py
@@ -31,10 +31,10 @@
     n_seq, n_head, q_hbm, k_hbm, v_hbm, decay_hbm, beta_hbm, gain_hbm, out_ref,
     q_ref, k_ref, v_ref, decay_ref, beta_ref, gain_ref,
     q_rows, k_rows, v_rows, out_rows, row_gate, beta_rows, kept_gate, terms_out, terms_in, solver_out, solver_in, query_out, query_in, offset,
-    prefix, slab_high, slab_low, slab_add, query_map, query_add,
+    prefix, slab_map, slab_add, front_map, chip_map, chip_add, entry, query_map, query_add,
     chain_in, chain_out, core_out, core_in,
     load_sem, terms_send, terms_recv, solver_send, solver_recv, query_send, query_recv,
-    chain_send, chain_recv, core_send, core_recv,
+    map_send, map_recv, entry_send, entry_recv, chain_send, chain_recv, core_send, core_recv,
 ):
     seq, me = lax.axis_index("seq"), lax.axis_index("head")
     tokens, heads, width = q_ref.shape
@@ -56,10 +56,13 @@
     barrier = pltpu.get_barrier_semaphore()
     for step in range(1, n_head):
         pl.semaphore_signal(barrier, inc=1, device_id=partner(step), device_id_type=MESH)
-    for side in (1, n_seq - 1):
+    odd = lax.rem(seq, 2)
+    mate = {"seq": seq + 1 - 2 * odd}
+    for ahead in (2, n_seq - 2):
         pl.semaphore_signal(
-            barrier, inc=1, device_id={"seq": lax.rem(seq + side, n_seq)}, device_id_type=MESH
-        )
+            barrier, inc=1, device_id={"seq": lax.rem(seq + ahead, n_seq)}, device_id_type=MESH
+        )
+    pl.semaphore_signal(barrier, inc=1, device_id=mate, device_id_type=MESH)
 
     size = PACK * tokens
     row = lax.broadcasted_iota(jnp.int32, (size, size), 0)
@@ -223,7 +226,7 @@
     order = list(range(1, n_head)) + [0]
     units = [(step, part) for step in order for part in range(own)]
     packs = [units[at : at + PACK] for at in range(0, len(units), PACK)]
-    pl.semaphore_wait(barrier, n_head + 1)
+    pl.semaphore_wait(barrier, n_head + 2)
     for step in order:
         store_terms(step)
     loads[4].wait()
@@ -301,18 +304,36 @@
                 change = jnp.concatenate([erasers, -pseudo], axis=1)
             decay = jnp.concatenate([decay, decay], axis=1)
             current[part] = current[part] * decay - dot(carried, change, TN)
-    for part in range(own):
-        high = current[part][:, :width].astype(BF16)
-        slab_high[part] = high
-        slab_low[part] = (current[part][:, :width] - high.astype(F32)).astype(BF16)
-        slab_add[part] = current[part][:, width:]
+    def map_copy(part):
+        return pltpu.make_async_remote_copy(
+            src_ref=slab_map.at[part], dst_ref=front_map.at[part],
+            send_sem=map_send.at[part], recv_sem=map_recv.at[part],
+            device_id=mate, device_id_type=MESH,
+        )
+
+    def entry_copy(part):
+        return pltpu.make_async_remote_copy(
+            src_ref=chain_in.at[part], dst_ref=entry.at[part],
+            send_sem=entry_send.at[part], recv_sem=entry_recv.at[part],
+            device_id=mate, device_id_type=MESH,
+        )
 
     def chain_copy(part):
         return pltpu.make_async_remote_copy(
             src_ref=chain_out.at[part], dst_ref=chain_in.at[part],
             send_sem=chain_send.at[part], recv_sem=chain_recv.at[part],
-            device_id={"seq": lax.rem(seq + 1, n_seq)}, device_id_type=MESH,
-        )
+            device_id={"seq": lax.rem(seq + 2, n_seq)}, device_id_type=MESH,
+        )
+
+    def keep(target, part, linear):
+        high = linear.astype(BF16)
+        target[part, 0] = high
+        target[part, 1] = (linear - high.astype(F32)).astype(BF16)
+
+    for part in range(own):
+        keep(slab_map, part, current[part][:, :width])
+        slab_map[part, 2] = current[part][:, width:].astype(BF16)
+        slab_add[part] = current[part][:, width:]
 
     def core_copy(step, part):
         slot = n_head - step
@@ -335,44 +356,93 @@
                 query_map[part, section, :] = mapped[:, :width].astype(BF16)
                 query_add[part, section, :] = mapped[:, width:]
 
-    def pass_on(part):
-        @pl.when(seq > 0)
-        def _():
-            chain_copy(part).wait_recv()
-
-        @pl.when(seq < n_seq - 1)
-        def _():
-            state = chain_in[part]
-            moved = dot(slab_high[part], state) + dot(slab_low[part], state)
-            chain_out[part] = (moved + slab_add[part]).astype(BF16)
-            chain_copy(part).start()
-
     def give_cores(part):
-        cores = dot(query_map[part], chain_in[part]) + query_add[part]
+        cores = dot(query_map[part], entry[part]) + query_add[part]
         core_out[part] = cores.astype(BF16).reshape(n_head, tokens, width)
         for step in range(1, n_head):
             core_copy(step, part).start()
 
-    @pl.when(seq == 0)
+    @pl.when(odd == 0)
     def _():
-        chain_in[...] = jnp.zeros_like(chain_in)
-
-    late = seq >= n_seq // 2
-
-    @pl.when(late)
+        for part in range(own):
+            map_copy(part).start()
+        map_queries()
+        for part in range(own):
+            entry_copy(part).wait_recv()
+            give_cores(part)
+        for part in range(own):
+            map_copy(part).wait_send()
+
+    first, last, late = seq < 2, seq >= n_seq - 2, seq >= n_seq // 2
+
+    def compose_chip():
+        for part in range(own):
+            map_copy(part).wait_recv()
+            high, low = slab_map[part, 0], slab_map[part, 1]
+            front, front_low, front_add = (front_map[part, at] for at in range(3))
+            linear = dot(high, front) + (dot(low, front) + dot(high, front_low))
+            keep(chip_map, part, linear)
+            chip_add[part] = dot(high, front_add) + dot(low, front_add) + slab_add[part]
+
+    def pass_on(part):
+        @pl.when(jnp.logical_not(first))
+        def _():
+            chain_copy(part).wait_recv()
+
+        @pl.when(jnp.logical_not(last))
+        def _():
+            state = chain_in[part]
+            moved = dot(chip_map[part, 0], state) + dot(chip_map[part, 1], state)
+            chain_out[part] = (moved + chip_add[part]).astype(BF16)
+            chain_copy(part).start()
+
+        entry_copy(part).start()
+
+    def enter(part):
+        state = chain_in[part]
+        moved = dot(front_map[part, 0], state) + dot(front_map[part, 1], state)
+        entry[part] = (moved + front_map[part, 2].astype(F32)).astype(BF16)
+        give_cores(part)
+
+    @pl.when(odd == 1)
     def _():
-        map_queries()
-        for part in range(own):
-            pass_on(part)
-            give_cores(part)
-
-    @pl.when(jnp.logical_not(late))
-    def _():
-        for part in range(own):
-            pass_on(part)
-        map_queries()
-        for part in range(own):
-            give_cores(part)
+        @pl.when(first)
+        def _():
+            chain_in[...] = jnp.zeros_like(chain_in)
+
+        compose_chip()
+
+        @pl.when(last)
+        def _():
+            map_queries()
+            for part in range(own):
+                pass_on(part)
+                if part:
+                    enter(part - 1)
+            enter(own - 1)
+
+        @pl.when(jnp.logical_not(last))
+        def _():
+            @pl.when(late)
+            def _():
+                map_queries()
+
+            for part in range(own):
+                pass_on(part)
+
+            @pl.when(jnp.logical_not(late))
+            def _():
+                map_queries()
+
+            for part in range(own):
+                enter(part)
+
+        for part in range(own):
+            entry_copy(part).wait_send()
+
+            @pl.when(jnp.logical_not(last))
+            def _():
+                chain_copy(part).wait_send()
 
     gain = gain_ref[...]
     for step in [0] + list(range(n_head - 1, 0, -1)):
@@ -394,11 +464,6 @@
         query_copy(step).wait_send()
         for part in range(own):
             core_copy(step, part).wait_send()
-
-    @pl.when(seq < n_seq - 1)
-    def _():
-        for part in range(own):
-            chain_copy(part).wait_send()
 
 
 def solution(mesh):
@@ -439,9 +504,12 @@
                 pltpu.VMEM((n_head, own * tokens, width), BF16),
                 pltpu.VMEM((n_head, own, tokens, width), F32),
                 pltpu.VMEM((own, n_head, width, 2 * width), BF16),
+                pltpu.VMEM((own, 3, width, width), BF16),
+                pltpu.VMEM((own, width, width), F32),
+                pltpu.VMEM((own, 3, width, width), BF16),
+                pltpu.VMEM((own, 2, width, width), BF16),
+                pltpu.VMEM((own, width, width), F32),
                 pltpu.VMEM((own, width, width), BF16),
-                pltpu.VMEM((own, width, width), BF16),
-                pltpu.VMEM((own, width, width), F32),
                 pltpu.VMEM((own, n_head * tokens, width), BF16),
                 pltpu.VMEM((own, n_head * tokens, width), F32),
                 pltpu.VMEM((own, width, width), BF16),
@@ -457,6 +525,10 @@
                 dma((n_head,)),
                 dma((own,)),
                 dma((own,)),
+                dma((own,)),
+                dma((own,)),
+                dma((own,)),
+                dma((own,)),
                 dma((n_head, own)),
                 dma((n_head, own)),
             ],

time: 32.6 us -> 31.1 us (0.954)
  the two profiles are of different devices: /device:TPU:25 before, /device:TPU:24 now
where the time goes in v4:
time: 31.1 us; the launch traced here: 30.9 us
  Pallas kernels  30.2 us (97%)
  local copies, waits for them, and re-layouts  0.71 us (2%)
    pallas_call x1, Pallas kernels, local(): pl.pallas_call(functools.partial(kernel, n_seq, n_head), out_shape=pltpu....  30.2 us
    unnamed x1, local copies, waits for them, and re-layouts  0.71 us

profile of v4, /device:TPU:24, one launch (start us, length us, event | category | flops | bytes accessed | tf_op | source)
XLA Modules:
  0.0 30.9 jit_solution(1212045418719617429)
XLA Ops:
  0.0 30.2 %gated_delta.1 = bf16[64,16,128]{2,1,0:T(8,128)(2,1)S(1)} custom-call(bf16[64,16,128]{2,1,0:T(8,128)(2,1)} %q_hbm.1, bf16[64,16,128]{2,1,0:T(8,128)(2,1)} %k_hbm.1, bf16[64,16,128]{2,1,0:T(8,128)(2,1)} %v_hbm.1, bf16[16,64]{1,0:T(8,128)(2,1)} %bitcast.3, bf16[16,64]{1,0:T(8,128)(2,1)} %bitcast.4, f32[1,128]{1,0:T(1,128)} %bitcast.5), custom_call_target="tpu_custom_call" | custom-call | tf_op jit(solution)/shard_map/gated_delta/pallas_call | solution.py:480
  30.2 0.7 %copy.8 = bf16[64,16,128]{2,1,0:T(8,128)(2,1)} copy(bf16[64,16,128]{2,1,0:T(8,128)(2,1)S(1)} %gated_delta.1) | data formatting | bytes 524288

commit v5 on v4

--- a/solution.py
+++ b/solution.py
@@ -127,12 +127,6 @@
         fourth = short([dot(a, a) for a in square])
         inverse = [x + dot(y, a) for x, y, a in zip(inverse, short(inverse), square)]
         inverse = [x + dot(y, a) for x, y, a in zip(inverse, short(inverse), fourth)]
-        grown = [jnp.exp(c) for c in cum]
-        wide = [k.astype(F32) for k in keys]
-        right = short([
-            jnp.concatenate([stack(v_rows, pack) * b, w * (g * b)], axis=1)
-            for pack, b, w, g in zip(ids, beta, wide, grown)
-        ])
         while block < tokens:
             between = same(2 * block) & ~same(block)
             corner = short([jnp.where(between, a, 0.0) for a in lower])
@@ -141,18 +135,16 @@
             block *= 2
             if block < tokens:
                 inverse = [x - dot(a, y) for x, a, y in zip(inverse, crossed, held)]
-        partly = [dot(x, r) for x, r in zip(held, right)]
-        solved = short([y - dot(a, z) for y, a, z in zip(partly, crossed, short(partly))])
         scales = [
             jnp.where(first_head, beta_rows[pl.ds(pack[0], 1), :], beta_rows[pl.ds(pack[1], 1), :])
             for pack in ids
         ]
-        solver = [
+        solver = short([
             (x - dot(a, y)) * b for x, a, y, b in zip(inverse, crossed, held, scales)
-        ]
+        ])
         return [
-            dict(units=pack, ids=i, spread=s, keys=k, solved=x, grown=g, solver=t)
-            for pack, i, s, k, x, g, t in zip(packs, ids, spread, keys, solved, grown, solver)
+            dict(units=pack, ids=i, spread=s, keys=k, cum=c, solver=t)
+            for pack, i, s, k, c, t in zip(packs, ids, spread, keys, cum, solver)
         ]
 
     def terms_copy(step):
@@ -206,17 +198,32 @@
                 if own == 1:
                     mine = (top, low)[at]
                     both = jnp.concatenate([mine[:, tokens:], mine[:, :tokens]], axis=1) + mine
-                    target[...] = both.astype(BF16)
+                    target[...] = both
                 elif at == 0:
                     to = part // 2 * tokens
-                    target[to : to + tokens, :] = (top + low).astype(BF16)
-
-    def query_terms(batch):
+                    target[to : to + tokens, :] = top + low
+
+    def score_terms(batch):
         queries = [stack(q_rows, data["ids"]).astype(BF16) for data in batch]
         scores = short([dot(q, d["keys"], NT) * d["spread"] for q, d in zip(queries, batch)])
-        mixed = [dot(s, d["solved"]) for s, d in zip(scores, batch)]
-        for q, m, d in zip(queries, mixed, batch):
-            through = (q.astype(F32) * d["grown"] - m[:, width:]).astype(BF16)
+        grown = [jnp.exp(d["cum"]) for d in batch]
+        right = [
+            jnp.concatenate(
+                [stack(v_rows, d["ids"]).astype(BF16), (d["keys"].astype(F32) * g).astype(BF16)],
+                axis=1,
+            )
+            for d, g in zip(batch, grown)
+        ]
+        solved = short([dot(d["solver"], r) for d, r in zip(batch, right)])
+        return [
+            dict(units=d["units"], gated=q.astype(F32) * g, scores=c, solved=x)
+            for d, q, g, c, x in zip(batch, queries, grown, scores, solved)
+        ]
+
+    def query_terms(batch):
+        mixed = [dot(d["scores"], d["solved"]) for d in batch]
+        for m, d in zip(mixed, batch):
+            through = (d["gated"] - m[:, width:]).astype(BF16)
             for at, (step, part) in enumerate(d["units"]):
                 section, to = slice(at * tokens, (at + 1) * tokens), part * tokens
                 target = query_in.at[me] if step == 0 else query_out.at[step]
@@ -229,9 +236,6 @@
     pl.semaphore_wait(barrier, n_head + 2)
     for step in order:
         store_terms(step)
-    loads[4].wait()
-    q_rows[...] = unit(q_ref[...]) * width ** (-0.5)
-    loads[5].wait()
     kept = []
     for at in range(0, len(packs), BATCH):
         batch = batch_terms(packs[at : at + BATCH])
@@ -239,10 +243,10 @@
         kept.append(batch)
     for step in range(1, n_head):
         solver_copy(step).start()
-    for batch in kept:
-        query_terms(batch)
-    for step in range(1, n_head):
-        query_copy(step).start()
+    loads[4].wait()
+    q_rows[...] = unit(q_ref[...]) * width ** (-0.5)
+    loads[5].wait()
+    scored = [score_terms(batch) for batch in kept]
 
     for step in range(1, n_head):
         terms_copy(step).wait_recv()
@@ -304,10 +308,11 @@
                 change = jnp.concatenate([erasers, -pseudo], axis=1)
             decay = jnp.concatenate([decay, decay], axis=1)
             current[part] = current[part] * decay - dot(carried, change, TN)
-    def map_copy(part):
-        return pltpu.make_async_remote_copy(
-            src_ref=slab_map.at[part], dst_ref=front_map.at[part],
-            send_sem=map_send.at[part], recv_sem=map_recv.at[part],
+    def map_copy(part, what):
+        section = (slice(0, 2), slice(2, 3))[what]
+        return pltpu.make_async_remote_copy(
+            src_ref=slab_map.at[part, section], dst_ref=front_map.at[part, section],
+            send_sem=map_send.at[what, part], recv_sem=map_recv.at[what, part],
             device_id=mate, device_id_type=MESH,
         )
 
@@ -334,6 +339,23 @@
         keep(slab_map, part, current[part][:, :width])
         slab_map[part, 2] = current[part][:, width:].astype(BF16)
         slab_add[part] = current[part][:, width:]
+
+    first, last, late = seq < 2, seq >= n_seq - 2, seq >= n_seq // 2
+
+    @pl.when(odd == 0)
+    def _():
+        for part in range(own):
+            map_copy(part, 1).start()
+
+        @pl.when(jnp.logical_not(first))
+        def _():
+            for part in range(own):
+                map_copy(part, 0).start()
+
+    for batch in scored:
+        query_terms(batch)
+    for step in range(1, n_head):
+        query_copy(step).start()
 
     def core_copy(step, part):
         slot = n_head - step
@@ -362,22 +384,15 @@
         for step in range(1, n_head):
             core_copy(step, part).start()
 
-    @pl.when(odd == 0)
-    def _():
-        for part in range(own):
-            map_copy(part).start()
-        map_queries()
-        for part in range(own):
-            entry_copy(part).wait_recv()
-            give_cores(part)
-        for part in range(own):
-            map_copy(part).wait_send()
-
-    first, last, late = seq < 2, seq >= n_seq - 2, seq >= n_seq // 2
+    def send_on(part):
+        @pl.when(jnp.logical_not(last))
+        def _():
+            chain_copy(part).start()
 
     def compose_chip():
         for part in range(own):
-            map_copy(part).wait_recv()
+            map_copy(part, 1).wait_recv()
+            map_copy(part, 0).wait_recv()
             high, low = slab_map[part, 0], slab_map[part, 1]
             front, front_low, front_add = (front_map[part, at] for at in range(3))
             linear = dot(high, front) + (dot(low, front) + dot(high, front_low))
@@ -385,9 +400,7 @@
             chip_add[part] = dot(high, front_add) + dot(low, front_add) + slab_add[part]
 
     def pass_on(part):
-        @pl.when(jnp.logical_not(first))
-        def _():
-            chain_copy(part).wait_recv()
+        chain_copy(part).wait_recv()
 
         @pl.when(jnp.logical_not(last))
         def _():
@@ -404,12 +417,42 @@
         entry[part] = (moved + front_map[part, 2].astype(F32)).astype(BF16)
         give_cores(part)
 
-    @pl.when(odd == 1)
+    @pl.when(odd == 0)
     def _():
+        map_queries()
+
         @pl.when(first)
         def _():
-            chain_in[...] = jnp.zeros_like(chain_in)
-
+            entry[...] = jnp.zeros_like(entry)
+
+        for part in range(own):
+            @pl.when(jnp.logical_not(first))
+            def _():
+                entry_copy(part).wait_recv()
+
+            give_cores(part)
+        for part in range(own):
+            map_copy(part, 1).wait_send()
+
+            @pl.when(jnp.logical_not(first))
+            def _():
+                map_copy(part, 0).wait_send()
+
+    @pl.when((odd == 1) & first)
+    def _():
+        for part in range(own):
+            map_copy(part, 1).wait_recv()
+            state = front_map[part, 2]
+            entry[part] = state
+            moved = dot(slab_map[part, 0], state) + dot(slab_map[part, 1], state)
+            chain_out[part] = (moved + slab_add[part]).astype(BF16)
+            send_on(part)
+        map_queries()
+        for part in range(own):
+            give_cores(part)
+
+    @pl.when((odd == 1) & jnp.logical_not(first))
+    def _():
         compose_chip()
 
         @pl.when(last)
@@ -440,9 +483,10 @@
         for part in range(own):
             entry_copy(part).wait_send()
 
-            @pl.when(jnp.logical_not(last))
-            def _():
-                chain_copy(part).wait_send()
+    @pl.when((odd == 1) & jnp.logical_not(last))
+    def _():
+        for part in range(own):
+            chain_copy(part).wait_send()
 
     gain = gain_ref[...]
     for step in [0] + list(range(n_head - 1, 0, -1)):
@@ -523,8 +567,8 @@
                 dma((n_head,)),
                 dma((n_head,)),
                 dma((n_head,)),
-                dma((own,)),
-                dma((own,)),
+                dma((2, own)),
+                dma((2, own)),
                 dma((own,)),
                 dma((own,)),
                 dma((own,)),

time: 31.1 us -> 29.3 us (0.942)
  Pallas kernels: 30.2 us -> 28.4 us
    pallas_call x1, Pallas kernels: 30.2 us -> 28.4 us  [local(): pl.pallas_call(functools.partial(kernel, n_seq, n_head), out_shape=pltpu....]
where the time goes in v5:
time: 29.3 us; the launch traced here: 29.1 us
  Pallas kernels  28.4 us (97%)
  local copies, waits for them, and re-layouts  0.71 us (2%)
    pallas_call x1, Pallas kernels, local(): pl.pallas_call(functools.partial(kernel, n_seq, n_head), out_shape=pltpu....  28.4 us
    unnamed x1, local copies, waits for them, and re-layouts  0.71 us

profile of v5, /device:TPU:24, one launch (start us, length us, event | category | flops | bytes accessed | tf_op | source)
XLA Modules:
  0.0 29.1 jit_solution(5925622389021149419)
XLA Ops:
  0.0 28.4 %gated_delta.1 = bf16[64,16,128]{2,1,0:T(8,128)(2,1)S(1)} custom-call(bf16[64,16,128]{2,1,0:T(8,128)(2,1)} %q_hbm.1, bf16[64,16,128]{2,1,0:T(8,128)(2,1)} %k_hbm.1, bf16[64,16,128]{2,1,0:T(8,128)(2,1)} %v_hbm.1, bf16[16,64]{1,0:T(8,128)(2,1)} %bitcast.3, bf16[16,64]{1,0:T(8,128)(2,1)} %bitcast.4, f32[1,128]{1,0:T(1,128)} %bitcast.5), custom_call_target="tpu_custom_call" | custom-call | tf_op jit(solution)/shard_map/gated_delta/pallas_call | solution.py:524
  28.4 0.7 %copy.8 = bf16[64,16,128]{2,1,0:T(8,128)(2,1)} copy(bf16[64,16,128]{2,1,0:T(8,128)(2,1)S(1)} %gated_delta.1) | data formatting | bytes 524288

commit v6 on v5

--- a/solution.py
+++ b/solution.py
@@ -44,8 +44,8 @@
     def partner(step):
         return {"head": lax.rem(me + step, n_head)}
 
-    sources = (decay_hbm, beta_hbm, k_hbm, v_hbm, q_hbm, gain_hbm)
-    targets = (decay_ref, beta_ref, k_ref, v_ref, q_ref, gain_ref)
+    sources = (v_hbm, k_hbm, decay_hbm, beta_hbm, q_hbm, gain_hbm)
+    targets = (v_ref, k_ref, decay_ref, beta_ref, q_ref, gain_ref)
     loads = [
         pltpu.make_async_copy(source, target, load_sem.at[at])
         for at, (source, target) in enumerate(zip(sources, targets))
@@ -81,25 +81,15 @@
     before = lax.broadcasted_iota(jnp.int32, (tokens, size), 0) <= token_of
     lane = lax.broadcasted_iota(jnp.int32, (tokens, heads), 1)
 
-    loads[0].wait()
-    log_rows = dot(decay_ref[...], jnp.where(before, 1.0, 0.0).astype(BF16))
-    row_gate[...] = log_rows
-    log_end = log_rows[:, size - 1 :]
-    first_half = lax.broadcasted_iota(jnp.int32, (heads, size), 1) < tokens
-    kept_gate[0] = jnp.exp(jnp.where(first_half, log_rows, log_end - log_rows))
-    kept_gate[1] = jnp.broadcast_to(jnp.exp(log_end), (heads, size))
-    cumulative = dot(jnp.where(row_t >= col_t, 1.0, 0.0).astype(BF16), decay_ref[...], NT)
-    loads[1].wait()
-    row_beta = dot(beta_ref[...], jnp.where(token_of == lax.broadcasted_iota(
-        jnp.int32, (tokens, size), 0), 1.0, 0.0).astype(BF16))
-    beta_rows[...] = row_beta
-    betas = dot(jnp.where(row_t == col_t, 1.0, 0.0).astype(BF16), beta_ref[...], NT)
-    loads[2].wait()
-    k_rows[...] = unit(k_ref[...])
-    loads[3].wait()
-    v_rows[...] = v_ref[...].astype(F32).reshape(-1, width)
     def stack(ref, ids):
         return jnp.concatenate([ref[pl.ds(i, tokens, stride=heads), :] for i in ids], axis=0)
+
+    def held_rows(first_row, pack):
+        kept_rows = []
+        for step, part in pack:
+            source = terms_in.at[me] if step == 0 else terms_out.at[step]
+            kept_rows.append(source[first_row + part * tokens : first_row + (part + 1) * tokens, :])
+        return jnp.concatenate(kept_rows, axis=0)
 
     def column(gate, i):
         picked = jnp.sum(jnp.where(lane == i, gate, 0.0), axis=1, keepdims=True)
@@ -115,7 +105,7 @@
             for pack in ids
         ]
         spread = [jnp.exp(jnp.where(within, c - a, -1e30)) for c, a in zip(cum, across)]
-        keys = [stack(k_rows, pack).astype(BF16) for pack in ids]
+        keys = [held_rows(rows, pack) for pack in packs]
         lower = [
             jnp.where(strict, dot(k, k, NT) * s, 0.0) * b for k, s, b in zip(keys, spread, beta)
         ]
@@ -147,10 +137,11 @@
             for pack, i, s, k, c, t in zip(packs, ids, spread, keys, cum, solver)
         ]
 
-    def terms_copy(step):
+    def terms_copy(step, what):
+        section = (slice(0, rows), slice(rows, 2 * rows + 16))[what]
         return pltpu.make_async_remote_copy(
-            src_ref=terms_out.at[step], dst_ref=terms_in.at[me],
-            send_sem=terms_send.at[step], recv_sem=terms_recv.at[step],
+            src_ref=terms_out.at[step, section], dst_ref=terms_in.at[me, section],
+            send_sem=terms_send.at[what, step], recv_sem=terms_recv.at[what, step],
             device_id=partner(step), device_id_type=MESH,
         )
 
@@ -170,14 +161,22 @@
 
     tail_row = lax.broadcasted_iota(jnp.int32, (16, width), 0)
 
-    def store_terms(step):
+    def store_values(step):
+        target = terms_in.at[me] if step == 0 else terms_out.at[step]
+        for part in range(own):
+            head, to = lax.rem(me + step, n_head) * own + part, part * tokens
+            from_head = pl.ds(head, tokens, stride=heads)
+            target[to : to + tokens, :] = v_rows[from_head, :].astype(BF16)
+        if step:
+            terms_copy(step, 0).start()
+
+    def store_keys(step):
         target = terms_in.at[me] if step == 0 else terms_out.at[step]
         tail = jnp.zeros((16, width), F32)
         for part in range(own):
             head, to = lax.rem(me + step, n_head) * own + part, part * tokens
             from_head = pl.ds(head, tokens, stride=heads)
-            target[to : to + tokens, :] = k_rows[from_head, :].astype(BF16)
-            target[rows + to : rows + to + tokens, :] = v_rows[from_head, :].astype(BF16)
+            target[rows + to : rows + to + tokens, :] = k_rows[from_head, :].astype(BF16)
             decay = kept_gate[1, pl.ds(head, 1), :]
             high = decay.astype(BF16).astype(F32)
             tail = jnp.where(tail_row == 3 * part, kept_gate[0, pl.ds(head, 1), :], tail)
@@ -185,7 +184,7 @@
             tail = jnp.where(tail_row == 3 * part + 2, decay - high, tail)
         target[2 * rows :, :] = tail.astype(BF16)
         if step:
-            terms_copy(step).start()
+            terms_copy(step, 1).start()
 
     pairs = max(own // 2, 1)
 
@@ -209,7 +208,7 @@
         grown = [jnp.exp(d["cum"]) for d in batch]
         right = [
             jnp.concatenate(
-                [stack(v_rows, d["ids"]).astype(BF16), (d["keys"].astype(F32) * g).astype(BF16)],
+                [held_rows(0, d["units"]), (d["keys"].astype(F32) * g).astype(BF16)],
                 axis=1,
             )
             for d, g in zip(batch, grown)
@@ -233,9 +232,28 @@
     order = list(range(1, n_head)) + [0]
     units = [(step, part) for step in order for part in range(own)]
     packs = [units[at : at + PACK] for at in range(0, len(units), PACK)]
+    loads[0].wait()
+    v_rows[...] = v_ref[...].astype(F32).reshape(-1, width)
     pl.semaphore_wait(barrier, n_head + 2)
     for step in order:
-        store_terms(step)
+        store_values(step)
+    loads[2].wait()
+    log_rows = dot(decay_ref[...], jnp.where(before, 1.0, 0.0).astype(BF16))
+    row_gate[...] = log_rows
+    log_end = log_rows[:, size - 1 :]
+    first_half = lax.broadcasted_iota(jnp.int32, (heads, size), 1) < tokens
+    kept_gate[0] = jnp.exp(jnp.where(first_half, log_rows, log_end - log_rows))
+    kept_gate[1] = jnp.broadcast_to(jnp.exp(log_end), (heads, size))
+    cumulative = dot(jnp.where(row_t >= col_t, 1.0, 0.0).astype(BF16), decay_ref[...], NT)
+    loads[3].wait()
+    row_beta = dot(beta_ref[...], jnp.where(token_of == lax.broadcasted_iota(
+        jnp.int32, (tokens, size), 0), 1.0, 0.0).astype(BF16))
+    beta_rows[...] = row_beta
+    betas = dot(jnp.where(row_t == col_t, 1.0, 0.0).astype(BF16), beta_ref[...], NT)
+    loads[1].wait()
+    k_rows[...] = unit(k_ref[...])
+    for step in order:
+        store_keys(step)
     kept = []
     for at in range(0, len(packs), BATCH):
         batch = batch_terms(packs[at : at + BATCH])
@@ -249,14 +267,15 @@
     scored = [score_terms(batch) for batch in kept]
 
     for step in range(1, n_head):
-        terms_copy(step).wait_recv()
+        terms_copy(step, 0).wait_recv()
+        terms_copy(step, 1).wait_recv()
     low_lane = lax.broadcasted_iota(jnp.int32, (tokens, size), 1) < tokens
     eye_t = row_t == col_t
     shrunk = []
     for group in range(n_head):
         tail = terms_in[group, 2 * rows :, :].astype(F32)
         for part in range(own):
-            keys = terms_in[group, part * tokens : (part + 1) * tokens, :]
+            keys = terms_in[group, rows + part * tokens : rows + (part + 1) * tokens, :]
             shrink = tail[3 * part : 3 * part + 1, tokens:]
             shrunk.append(dot(jnp.where(eye_t, shrink, 0.0).astype(BF16), keys).astype(BF16))
     for step in range(1, n_head):
@@ -279,8 +298,8 @@
                 diagonal = lambda t: t[:, :tokens].astype(BF16)
             section = slice(pair * many * tokens, (pair + 1) * many * tokens)
             beyond = slice(rows + section.start, rows + section.stop)
-            erasers = dot(diagonal(solver * grow), terms_in[group, section, :]).astype(BF16)
-            pseudo = dot(diagonal(solver), terms_in[group, beyond, :]).astype(BF16)
+            erasers = dot(diagonal(solver * grow), terms_in[group, beyond, :]).astype(BF16)
+            pseudo = dot(diagonal(solver), terms_in[group, section, :]).astype(BF16)
             for at in range(many):
                 erasers_of.append(erasers[at * tokens : (at + 1) * tokens])
                 pseudo_of.append(pseudo[at * tokens : (at + 1) * tokens])
@@ -503,7 +522,8 @@
     out_ref[...] = out_rows[...].reshape(tokens, heads, width).astype(BF16)
 
     for step in range(1, n_head):
-        terms_copy(step).wait_send()
+        terms_copy(step, 0).wait_send()
+        terms_copy(step, 1).wait_send()
         solver_copy(step).wait_send()
         query_copy(step).wait_send()
         for part in range(own):
@@ -561,8 +581,8 @@
                 pltpu.VMEM((own, n_head, tokens, width), BF16),
                 pltpu.VMEM((n_head, own, tokens, width), BF16),
                 dma((6,)),
-                dma((n_head,)),
-                dma((n_head,)),
+                dma((2, n_head)),
+                dma((2, n_head)),
                 dma((n_head,)),
                 dma((n_head,)),
                 dma((n_head,)),

time: 29.3 us -> 29.2 us (level)
  no operation moved by 1% of the time
where the time goes in v6:
time: 29.2 us; the launch traced here: 29.1 us
  Pallas kernels  28.4 us (97%)
  local copies, waits for them, and re-layouts  0.71 us (2%)
    pallas_call x1, Pallas kernels, local(): pl.pallas_call(functools.partial(kernel, n_seq, n_head), out_shape=pltpu....  28.4 us
    unnamed x1, local copies, waits for them, and re-layouts  0.71 us

profile of v6, /device:TPU:24, one launch (start us, length us, event | category | flops | bytes accessed | tf_op | source)
XLA Modules:
  0.0 29.1 jit_solution(2572376147455092190)
XLA Ops:
  0.0 28.4 %gated_delta.1 = bf16[64,16,128]{2,1,0:T(8,128)(2,1)S(1)} custom-call(bf16[64,16,128]{2,1,0:T(8,128)(2,1)} %q_hbm.1, bf16[64,16,128]{2,1,0:T(8,128)(2,1)} %k_hbm.1, bf16[64,16,128]{2,1,0:T(8,128)(2,1)} %v_hbm.1, bf16[16,64]{1,0:T(8,128)(2,1)} %bitcast.3, bf16[16,64]{1,0:T(8,128)(2,1)} %bitcast.4, f32[1,128]{1,0:T(1,128)} %bitcast.5), custom_call_target="tpu_custom_call" | custom-call | tf_op jit(solution)/shard_map/gated_delta/pallas_call | solution.py:544
  28.4 0.7 %copy.8 = bf16[64,16,128]{2,1,0:T(8,128)(2,1)} copy(bf16[64,16,128]{2,1,0:T(8,128)(2,1)S(1)} %gated_delta.1) | data formatting | bytes 524288

commit v7 on v6

--- a/solution.py
+++ b/solution.py
@@ -265,6 +265,10 @@
     q_rows[...] = unit(q_ref[...]) * width ** (-0.5)
     loads[5].wait()
     scored = [score_terms(batch) for batch in kept]
+    for batch in scored:
+        query_terms(batch)
+    for step in range(1, n_head):
+        query_copy(step).start()
 
     for step in range(1, n_head):
         terms_copy(step, 0).wait_recv()
@@ -370,11 +374,6 @@
         def _():
             for part in range(own):
                 map_copy(part, 0).start()
-
-    for batch in scored:
-        query_terms(batch)
-    for step in range(1, n_head):
-        query_copy(step).start()
 
     def core_copy(step, part):
         slot = n_head - step

time: 29.2 us -> 30.1 us (1.031)
  Pallas kernels: 28.4 us -> 29.2 us
    pallas_call x1, Pallas kernels: 28.4 us -> 29.2 us  [local(): pl.pallas_call(functools.partial(kernel, n_seq, n_head), out_shape=pltpu....]
where the time goes in v7:
time: 30.1 us; the launch traced here: 30 us
  Pallas kernels  29.2 us (97%)
  local copies, waits for them, and re-layouts  0.71 us (2%)
    pallas_call x1, Pallas kernels, local(): pl.pallas_call(functools.partial(kernel, n_seq, n_head), out_shape=pltpu....  29.2 us
    unnamed x1, local copies, waits for them, and re-layouts  0.71 us

profile of v7, /device:TPU:24, one launch (start us, length us, event | category | flops | bytes accessed | tf_op | source)
XLA Modules:
  0.0 30.0 jit_solution(14116643365091047063)
XLA Ops:
  0.0 29.2 %gated_delta.1 = bf16[64,16,128]{2,1,0:T(8,128)(2,1)S(1)} custom-call(bf16[64,16,128]{2,1,0:T(8,128)(2,1)} %q_hbm.1, bf16[64,16,128]{2,1,0:T(8,128)(2,1)} %k_hbm.1, bf16[64,16,128]{2,1,0:T(8,128)(2,1)} %v_hbm.1, bf16[16,64]{1,0:T(8,128)(2,1)} %bitcast.3, bf16[16,64]{1,0:T(8,128)(2,1)} %bitcast.4, f32[1,128]{1,0:T(1,128)} %bitcast.5), custom_call_target="tpu_custom_call" | custom-call | tf_op jit(solution)/shard_map/gated_delta/pallas_call | solution.py:543
  29.3 0.7 %copy.8 = bf16[64,16,128]{2,1,0:T(8,128)(2,1)} copy(bf16[64,16,128]{2,1,0:T(8,128)(2,1)S(1)} %gated_delta.1) | data formatting | bytes 524288

commit v8 on v6

--- a/solution.py
+++ b/solution.py
@@ -261,10 +261,6 @@
         kept.append(batch)
     for step in range(1, n_head):
         solver_copy(step).start()
-    loads[4].wait()
-    q_rows[...] = unit(q_ref[...]) * width ** (-0.5)
-    loads[5].wait()
-    scored = [score_terms(batch) for batch in kept]
 
     for step in range(1, n_head):
         terms_copy(step, 0).wait_recv()
@@ -361,8 +357,7 @@
 
     first, last, late = seq < 2, seq >= n_seq - 2, seq >= n_seq // 2
 
-    @pl.when(odd == 0)
-    def _():
+    def hand_over():
         for part in range(own):
             map_copy(part, 1).start()
 
@@ -371,10 +366,35 @@
             for part in range(own):
                 map_copy(part, 0).start()
 
+    @pl.when((odd == 0) & jnp.logical_not(late))
+    def _():
+        hand_over()
+
+    @pl.when((odd == 1) & first)
+    def _():
+        for part in range(own):
+            map_copy(part, 1).wait_recv()
+            state = front_map[part, 2]
+            entry[part] = state
+            moved = dot(slab_map[part, 0], state) + dot(slab_map[part, 1], state)
+            chain_out[part] = (moved + slab_add[part]).astype(BF16)
+
+            @pl.when(jnp.logical_not(last))
+            def _():
+                chain_copy(part).start()
+
+    loads[4].wait()
+    q_rows[...] = unit(q_ref[...]) * width ** (-0.5)
+    loads[5].wait()
+    scored = [score_terms(batch) for batch in kept]
     for batch in scored:
         query_terms(batch)
     for step in range(1, n_head):
         query_copy(step).start()
+
+    @pl.when((odd == 0) & late)
+    def _():
+        hand_over()
 
     def core_copy(step, part):
         slot = n_head - step
@@ -403,11 +423,6 @@
         for step in range(1, n_head):
             core_copy(step, part).start()
 
-    def send_on(part):
-        @pl.when(jnp.logical_not(last))
-        def _():
-            chain_copy(part).start()
-
     def compose_chip():
         for part in range(own):
             map_copy(part, 1).wait_recv()
@@ -459,13 +474,6 @@
 
     @pl.when((odd == 1) & first)
     def _():
-        for part in range(own):
-            map_copy(part, 1).wait_recv()
-            state = front_map[part, 2]
-            entry[part] = state
-            moved = dot(slab_map[part, 0], state) + dot(slab_map[part, 1], state)
-            chain_out[part] = (moved + slab_add[part]).astype(BF16)
-            send_on(part)
         map_queries()
         for part in range(own):
             give_cores(part)

time: 29.2 us -> 30.4 us (1.041)
  the two profiles are of different devices: /device:TPU:24 before, /device:TPU:0 now
where the time goes in v8:
time: 30.4 us; the launch traced here: 30.3 us
  Pallas kernels  29.6 us (97%)
  local copies, waits for them, and re-layouts  0.71 us (2%)
    pallas_call x1, Pallas kernels, local(): pl.pallas_call(functools.partial(kernel, n_seq, n_head), out_shape=pltpu....  29.6 us
    unnamed x1, local copies, waits for them, and re-layouts  0.71 us

profile of v8, /device:TPU:0, one launch (start us, length us, event | category | flops | bytes accessed | tf_op | source)
XLA Modules:
  0.0 30.3 jit_solution(4713768677451266409)
XLA Ops:
  0.0 29.6 %gated_delta.1 = bf16[64,16,128]{2,1,0:T(8,128)(2,1)S(1)} custom-call(bf16[64,16,128]{2,1,0:T(8,128)(2,1)} %q_hbm.1, bf16[64,16,128]{2,1,0:T(8,128)(2,1)} %k_hbm.1, bf16[64,16,128]{2,1,0:T(8,128)(2,1)} %v_hbm.1, bf16[16,64]{1,0:T(8,128)(2,1)} %bitcast.3, bf16[16,64]{1,0:T(8,128)(2,1)} %bitcast.4, f32[1,128]{1,0:T(1,128)} %bitcast.5), custom_call_target="tpu_custom_call" | custom-call | tf_op jit(solution)/shard_map/gated_delta/pallas_call | solution.py:552
  29.6 0.7 %copy.8 = bf16[64,16,128]{2,1,0:T(8,128)(2,1)} copy(bf16[64,16,128]{2,1,0:T(8,128)(2,1)S(1)} %gated_delta.1) | data formatting | bytes 524288
